TPU v7x, 512 devices: a whole 4x4x16 slice. The times are simulated.
512 devices in a mesh: fsdp: 64 (over z, y), img: 8 (over x, core).
Axes of the slice: x: 4, y: 4, z: 16, core: 2. Of those that a mesh axis runs over, the one named last changes fastest.
Arguments:
- tokens: bfloat16 [2048, 8192], P('fsdp', 'img'), may hold values from -6 to 6
- norm_gain: float32 [8192], P('img'), may hold values from 0.5 to 2
- w_query: bfloat16 [8192, 8192], P('img', 'fsdp'), may hold values from -0.0625 to 0.0625
- query_gain: float32 [128], replicated, may hold values from 0.5 to 2
- key_cache: bfloat16 [64, 8192, 1024], P('fsdp', 'img'), may hold values from -96 to 96
- value_cache: bfloat16 [64, 8192, 1024], P('fsdp', 'img'), may hold values from -48 to 48
- block_mask: int32 [2048, 8], P('fsdp'), may hold values from 0 to 1, as said below
- image_counts: int32 [512], P('fsdp'), may hold values from 1 to 2
- image_slot: int32 [512, 2], P('fsdp'), may hold values from 0 to 15, as said below
- attn_gate: float32 [1], replicated, may hold values from 0.8 to 2
- w_out: bfloat16 [8192, 8192], P('img', 'fsdp'), may hold values from -0.0625 to 0.0625
Outputs:
- mixed: bfloat16 [2048, 8192], P('img', 'fsdp')
Inputs may be any that keep to these rules, and one draw needn't show every extreme that they name: For k < image_counts[s], image k of sequence s is cached in rows image_slot[s, k] * 512 to (image_slot[s, k] + 1) * 512 - 1 of its group's caches; these entries are distinct within a group. Entries with k >= image_counts[s] name no image. `block_mask`: entry 0 of every row is 1: every text position attends the first key block of its sequence's first image.
All inputs are finite; a program needn't handle non-finite values.
Results may differ from a plain program's by a relative error of at most 0.0085.
The roundings to bfloat16 on the way count: a program that leaves them out, or rounds other values in their place, can miss the bound.
Values may be sent and summed in bfloat16 or wider, within the bound.
No kernel may reach another device: no remote copies, remote signals or barrier semaphores. Data moves between devices by JAX's collectives and lax.ppermute only.
A program may use at most 64 MiB of HBM per device.

v0:
```python
import jax
import jax.numpy as jnp
from jax import lax
from jax.sharding import PartitionSpec as P

H = 64
KVH = 8
HD = 128
IMG_BLK = 4
BLOCK_TOK = 128
IMG_TOK = 512


NEGATIVE = -1e30
EPSILON = 1e-05


def joined(value, axis, join):
    pieces = jax.tree.map(lambda part: lax.all_gather(part, axis), value)
    head = jax.tree.map(lambda part: part[0], pieces)
    tail = jax.tree.map(lambda part: part[1:], pieces)
    total, _ = lax.scan(lambda total, section: (join(total, section), None), head, tail)
    return total


def pair_merge(first, second):
    peak_first, total_first, weighted_first = first
    peak_second, total_second, weighted_second = second
    peak = jnp.maximum(peak_first, peak_second)
    factor_first = jnp.exp(peak_first - peak)
    factor_second = jnp.exp(peak_second - peak)
    total = total_first * factor_first + total_second * factor_second
    weighted = weighted_first * factor_first[..., None] + weighted_second * factor_second[..., None]
    return (peak, total, weighted)


def head_norm(query_raw, query_gain):
    row_count, columns = query_raw.shape
    per_head = query_raw.reshape(row_count, columns // HD, HD)
    inverse = lax.rsqrt(jnp.mean(per_head * per_head, axis=-1, keepdims=True) + EPSILON)
    return (per_head * inverse * query_gain).reshape(row_count, columns).astype(jnp.bfloat16)


def attend(query_four, keys, values, allowed):
    scores = jnp.einsum(
        "tkgd,skd->tkgs", query_four, keys, preferred_element_type=jnp.float32
    ) * HD ** (-0.5)
    visible = allowed[:, None, None, :]
    peak = jnp.max(jnp.where(visible, scores, NEGATIVE), axis=-1)
    expo = jnp.where(visible, jnp.exp(scores - peak[..., None]), 0.0)
    total = jnp.sum(expo, axis=-1)
    weighted = jnp.einsum(
        "tkgs,skd->tkgd", expo.astype(jnp.bfloat16), values, preferred_element_type=jnp.float32
    )
    row_count = query_four.shape[0]
    head_count = query_four.shape[1] * query_four.shape[2]
    return (
        peak.reshape(row_count, head_count),
        total.reshape(row_count, head_count),
        weighted.reshape(row_count, head_count, HD),
    )


def on_device(
    tokens,
    norm_gain,
    w_query,
    query_gain,
    key_cache,
    value_cache,
    block_mask,
    image_counts,
    image_slot,
    attn_gate,
    w_out,
):
    scaled = (tokens.astype(jnp.float32) * norm_gain).astype(jnp.bfloat16)
    owner = lax.axis_index("img")
    owners = lax.axis_size("img")
    partial_query = jnp.dot(
        lax.all_gather(scaled, "fsdp", axis=0, tiled=True),
        w_query,
        preferred_element_type=jnp.float32,
    )
    query_raw = lax.psum(partial_query, "img")
    query = head_norm(query_raw, query_gain)
    query = lax.all_to_all(query, "fsdp", split_axis=0, concat_axis=1, tiled=True)
    group_rows = query.shape[0]
    query_four = query.reshape(group_rows, KVH, H // KVH, HD)
    slots_here = key_cache.shape[1] // IMG_TOK
    slot_numbers = owner * slots_here + jnp.arange(slots_here, dtype=jnp.int32)
    live = jnp.arange(image_slot.shape[1], dtype=jnp.int32)[None, :] < image_counts[:, None]
    match = (image_slot[:, :, None] == slot_numbers[None, None, :]) & live[:, :, None]
    match = jnp.repeat(match, group_rows // image_counts.shape[0], axis=0)
    marked = block_mask.reshape(group_rows, image_slot.shape[1], IMG_BLK) == 1
    allowed = jnp.any(match[:, :, :, None] & marked[:, :, None, :], axis=1)
    allowed = jnp.repeat(allowed.reshape(group_rows, slots_here * IMG_BLK), BLOCK_TOK, axis=1)
    keys = key_cache[0].reshape(-1, KVH, HD)
    values = value_cache[0].reshape(-1, KVH, HD)
    row_peak, row_total, weighted = attend(query_four, keys, values, allowed)
    heads_owned = H // owners
    row_peak, row_total, weighted = joined((row_peak, row_total, weighted), "img", pair_merge)
    own_total = lax.dynamic_slice_in_dim(row_total, owner * heads_owned, heads_owned, 1)
    own_weighted = lax.dynamic_slice_in_dim(weighted, owner * heads_owned, heads_owned, 1)
    attended = own_weighted / own_total[..., None]
    attended = attended.reshape(group_rows, heads_owned * HD).astype(jnp.bfloat16)
    partial_out = jnp.dot(
        lax.all_gather(attended, "fsdp", axis=0, tiled=True),
        w_out,
        preferred_element_type=jnp.float32,
    )
    summed = lax.psum_scatter(partial_out, "img", scatter_dimension=0, tiled=True)
    return (jnp.tanh(attn_gate[0]) * summed).astype(jnp.bfloat16)


def solution(mesh):
    placed = (
        P("fsdp", "img"),
        P("img"),
        P("img", "fsdp"),
        P(),
        P("fsdp", "img", None),
        P("fsdp", "img", None),
        P("fsdp", None),
        P("fsdp"),
        P("fsdp", None),
        P(),
        P("img", "fsdp"),
    )
    return jax.shard_map(
        on_device, mesh=mesh, in_specs=placed, out_specs=P("img", "fsdp"), check_vma=False
    )
```

profile of v0, /device:TPU:1, one launch (start us, length us, event | category | flops | bytes accessed | tf_op | source)
XLA Modules:
  0.0 563.6 jit_solution(12561509785442292527)
XLA Ops:
  6.6 1.6 multiply_convert_fusion.2
  8.2 0.0 all-reduce.2.cloned.1.call-start
  8.2 145.9 %all-gather.4.cloned.1.call-done = bf16[2048,1024]{1,0:T(8,128)(2,1)} async-done(((bf16[32,1024]{1,0:T(8,128)(2,1)}), bf16[2048,1024]{1,0:T(8,128)(2,1)}) %all-gather.4.cloned.1.call-update) | async-done | bytes 4194320 | tf_op jit(solution)/shard_map/all_gather | solution.py:81
  154.2 4.4 fusion.26
  158.6 79.1 %all-reduce.2.cloned.1.call-done = f32[2048,128]{1,0:T(8,128)} async-done(((f32[2048,128]{1,0:T(8,128)}), f32[2048,128]{1,0:T(8,128)}) %all-reduce.2.cloned.1.call-update) | async-done | bytes 1048592 | tf_op jit(solution)/shard_map/psum | solution.py:85
  237.7 1.6 multiply_reduce_fusion
  239.3 2.4 multiply_convert_fusion
  241.6 14.9 %all-to-all-start = ((bf16[64,32,128]{2,1,0:T(8,128)(2,1)}), bf16[64,32,128]{2,1,0:T(8,128)(2,1)S(1)}, u32[]{:S(2)}, u32[]{:S(2)}) async-start(bf16[64,32,128]{2,1,0:T(8,128)(2,1)} %bitcast.6), calls=%async_computation | async-start | bytes 1048576 | tf_op jit(solution)/shard_map/all_to_all | solution.py:87
  256.6 0.0 all-gather.6.cloned.1.call-start
  256.7 0.1 compare_and_fusion
  256.7 0.1 broadcast_in_dim.39
  256.8 0.1 and.26
  256.9 0.1 copy.42
  257.0 0.1 broadcast_in_dim.40
  257.2 2.2 copy.60
  259.4 3.6 copy.61
  262.9 21.8 %all-to-all-done = bf16[64,32,128]{2,1,0:T(8,128)(2,1)S(1)} async-done(((bf16[64,32,128]{2,1,0:T(8,128)(2,1)}), bf16[64,32,128]{2,1,0:T(8,128)(2,1)S(1)}, u32[]{:S(2)}, u32[]{:S(2)}) %all-to-all-start) | async-done | bytes 524320 | tf_op jit(solution)/shard_map/all_to_all | solution.py:87
  284.7 2.1 fusion.3
  286.8 2.1 fusion.17
  288.9 1.2 copy-done.1
  290.0 1.1 copy.78
  291.2 0.0 all-gather.8.cloned.1.call-start
  291.2 0.1 copy.46
  291.3 0.1 copy.47
  291.4 4.7 fusion.7
  296.1 0.1 copy.48
  296.2 0.1 copy.49
  296.3 18.6 %all_gather.16 = f32[8,32,64]{2,1,0:T(8,128)S(1)} all-gather(f32[1,32,64]{2,1,0:T(8,128)S(1)} %copy.47), channel_id=1, replica_groups=mesh['fsdp'=64,'img'=8] {'img'}, dimensions={0}, use_global_device_ids=true | all-gather | bytes 73728 | tf_op jit(solution)/shard_map/all_gather | solution.py:19
  314.9 13.4 %all_gather.17 = f32[8,32,64]{2,1,0:T(8,128)S(1)} all-gather(f32[1,32,64]{2,1,0:T(8,128)S(1)} %copy.49), channel_id=1, replica_groups=mesh['fsdp'=64,'img'=8] {'img'}, dimensions={0}, use_global_device_ids=true | all-gather | bytes 73728 | tf_op jit(solution)/shard_map/all_gather | solution.py:19
  328.3 18.7 %all-gather.6.cloned.1.call-done = f32[8,32,64,128]{3,2,1,0:T(8,128)} async-done(((f32[1,32,64,128]{3,2,1,0:T(8,128)}), f32[8,32,64,128]{3,2,1,0:T(8,128)}) %all-gather.6.cloned.1.call-update) | async-done | bytes 8388624 | tf_op jit(solution)/shard_map/all_gather | solution.py:19
  347.0 1.3 slice_bitcast_fusion
  348.3 7.5 %slice.29 = f32[7,32,64,128]{3,2,1,0:T(8,128)} slice(f32[8,32,64,128]{3,2,1,0:T(8,128)} %all-gather.6.cloned.1.call-done), slice={[1:8], [0:32], [0:64], [0:128]} | slice | bytes 14680064 | tf_op jit(solution)/shard_map/slice | solution.py:21
  355.8 15.7 %while.14 = (s32[]{:T(128)}, f32[32,64]{1,0:T(8,128)S(1)}, f32[32,64]{1,0:T(8,128)S(1)}, f32[32,64,128]{2,1,0:T(8,128)S(1)}, f32[7,32,64]{2,1,0:T(8,128)S(1)}, /...) while((s32[]{:T(128)}, f32[32,64]{1,0:T(8,128)S(1)}, f32[32,64]{1,0:T(8,128)S(1)}, ...), condition=%wide.region_6.7_spmd, body=%wide.region_5.6_spmd.sunk | while | flops 798722 | bytes 3227749 | solution.py:22
  355.8 2.2 fusion.35
  358.1 2.2 fusion.35
  360.3 2.2 fusion.35
  362.5 2.2 fusion.35
  364.8 2.2 fusion.35
  367.0 2.2 fusion.35
  369.3 2.2 fusion.35
  371.5 0.1 constant_dynamic-slice_fusion
  371.5 0.1 divide_convert_fusion
  371.6 0.6 copy.80
  372.3 0.0 reduce-scatter.2.cloned.1.call-start
  372.4 138.0 %all-gather.8.cloned.1.call-done = bf16[2048,1024]{1,0:T(8,128)(2,1)} async-done(((bf16[32,1024]{1,0:T(8,128)(2,1)}), bf16[2048,1024]{1,0:T(8,128)(2,1)}) %all-gather.8.cloned.1.call-update) | async-done | bytes 4194320 | tf_op jit(solution)/shard_map/all_gather | solution.py:108
  510.4 4.4 fusion.27
  515.5 40.0 %reduce-scatter.2.cloned.1.call-done = f32[256,128]{1,0:T(8,128)} async-done(((f32[2048,128]{1,0:T(8,128)}), f32[256,128]{1,0:T(8,128)}) %reduce-scatter.2.cloned.1.call-update) | async-done | bytes 131088 | tf_op jit(solution)/shard_map/reduce_scatter | solution.py:112
  555.5 1.5 multiply_convert_fusion.1
  (38 shorter events, 0.4 us)
Async XLA Ops:
  6.5 147.6 %copy-start = (bf16[1024,128]{1,0:T(8,128)(2,1)S(1)}, bf16[1024,128]{1,0:T(8,128)(2,1)}, u32[]{:S(2)}) copy-start(bf16[1024,128]{1,0:T(8,128)(2,1)} %param.15) | copy-start | bytes 786436
  6.5 232.7 %copy-start.6 = (f32[128]{0:T(128)S(1)}, f32[128]{0:T(128)}, u32[]{:S(2)}) copy-start(f32[128]{0:T(128)} %param.16) | copy-start | bytes 1540
  6.5 250.1 %copy-start.7 = (s32[8]{0:T(128)S(1)}, s32[8]{0:T(128)}, u32[]{:S(2)}) copy-start(s32[8]{0:T(128)} %param.20) | copy-start | bytes 100
  6.5 250.1 %copy-start.5 = (s32[8,2]{0,1:T(2,128)S(1)}, s32[8,2]{0,1:T(2,128)}, u32[]{:S(2)}) copy-start(s32[8,2]{0,1:T(2,128)} %param.21) | copy-start | bytes 196
  6.5 250.4 %copy-start.4 = (s32[32,8]{0,1:T(8,128)S(1)}, s32[32,8]{0,1:T(8,128)}, u32[]{:S(2)}) copy-start(s32[32,8]{0,1:T(8,128)} %param.19) | copy-start | bytes 3076
  6.5 147.6 %all-gather.4.cloned.1.call-start = ((), (), s32[]{:S(2)}) async-start(), calls=%async_computation.2 | async-start | bytes 4259840 | tf_op jit(solution)/shard_map/all_gather | solution.py:81
  8.2 229.5 %all-reduce.2.cloned.1.call-start = ((), (), s32[]{:S(2)}) async-start(), calls=%async_computation.3 | async-start | bytes 2097152 | tf_op jit(solution)/shard_map/psum | solution.py:85
  241.6 43.1 %all-to-all-start = ((bf16[64,32,128]{2,1,0:T(8,128)(2,1)}), bf16[64,32,128]{2,1,0:T(8,128)(2,1)S(1)}, u32[]{:S(2)}, u32[]{:S(2)}) async-start(bf16[64,32,128]{2,1,0:T(8,128)(2,1)} %bitcast.6), calls=%async_computation | async-start | bytes 1048576 | tf_op jit(solution)/shard_map/all_to_all | solution.py:87
  256.6 90.4 %all-gather.6.cloned.1.call-start = ((), (), s32[]{:S(2)}) async-start(), calls=%async_computation.4 | async-start | bytes 9437184 | tf_op jit(solution)/shard_map/all_gather | solution.py:19
  284.7 2.1 copy-start.2
  286.8 3.2 copy-start.1
  291.2 219.2 %all-gather.8.cloned.1.call-start = ((), (), s32[]{:S(2)}) async-start(), calls=%async_computation.5 | async-start | bytes 4259840 | tf_op jit(solution)/shard_map/all_gather | solution.py:108
  355.8 154.6 %copy-start.3 = (bf16[1024,128]{1,0:T(8,128)(2,1)S(1)}, bf16[1024,128]{1,0:T(8,128)(2,1)}, u32[]{:S(2)}) copy-start(bf16[1024,128]{1,0:T(8,128)(2,1)} %param.23) | copy-start | bytes 786436
  372.3 183.2 %reduce-scatter.2.cloned.1.call-start = ((), (), s32[]{:S(2)}) async-start(), calls=%async_computation.6 | async-start | bytes 1179648 | tf_op jit(solution)/shard_map/reduce_scatter | solution.py:112
Sparse Core Ops, SparseCore 0:
  10.3 143.7 all-gather.3
  158.7 78.9 all-reduce.1
  291.3 55.6 all-gather.5
  372.4 137.8 all-gather.7
  514.9 40.5 reduce-scatter.1
where the time goes:
time: 565 us; the launch traced here: 564 us
  waiting for transfers between devices  444 us (79%)
  blocking collectives  32 us (6%)
  other arithmetic  27.5 us (5%)
  local copies, waits for them, and re-layouts  18.3 us (3%)
  starting transfers between devices  15.1 us (3%)
  between operations  14 us (2%)
  matrix products  12.9 us (2%)
    all_gather x1, waiting for transfers between devices, on_device(): lax.all_gather(scaled, 'fsdp', axis=0, tiled=True)  146 us
    all_gather x1, waiting for transfers between devices, on_device(): lax.all_gather(attended, 'fsdp', axis=0, tiled=True)  138 us
    psum x1, waiting for transfers between devices, on_device(): query_raw = lax.psum(partial_query, 'img')  79.1 us
    reduce_scatter x1, waiting for transfers between devices, on_device(): lax.psum_scatter(partial_out, 'img', scatter_dimension=0, tiled=True)  40 us
    all_gather x2, blocking collectives, joined(): pieces = jax.tree.map(lambda part: lax.all_gather(part, axis), value)  32 us
    all_to_all x1, waiting for transfers between devices, on_device(): lax.all_to_all(query, 'fsdp', split_axis=0, concat_axis=1, tiled=True)  21.8 us
    all_gather x1, waiting for transfers between devices, joined(): pieces = jax.tree.map(lambda part: lax.all_gather(part, axis), value)  18.7 us
    add x7, other arithmetic, pair_merge(): weighted_first * factor_first[..., None]  15.4 us
  transfers between devices with their start and end apart: 6, of which 6 were waited for; matrix products, arithmetic and copies ran while one was open for 2% of the time, Pallas kernels for 0%

commit v1 on v0

v1 whole, which is shorter than its diff:
```python
import functools

import jax
import jax.numpy as jnp
from jax import lax
from jax.experimental import pallas as pl
from jax.experimental.pallas import tpu as pltpu
from jax.sharding import Mesh
from jax.sharding import PartitionSpec as P

H = 64
KVH = 8
HD = 128
IMG_BLK = 4
BLOCK_TOK = 128
IMG_TOK = 512
STEPS = 4

NEGATIVE = -1e30
EPSILON = 1e-05

BF16 = jnp.bfloat16
F32 = jnp.float32
MIB = 1 << 20

AXES = ("j", "s", "y", "x", "c")
SIZES = (8, 2, 4, 4, 2)
ZED = ("j", "s")
IMG = ("x", "c")
FSDP = ("j", "s", "y")
MAIN = 896

SMEM = pl.BlockSpec(memory_space=pltpu.SMEM)


def cost(flops, size, exps=0):
    return pl.CostEstimate(flops=flops, bytes_accessed=size, transcendentals=exps)


def query_product(main, rest, weights):
    def kernel(main_ref, rest_ref, weight_ref, out_ref):
        product = jnp.dot(main_ref[...], weight_ref[0, :MAIN], preferred_element_type=F32)
        product += jnp.dot(
            rest_ref[...].reshape(512, 1024 - MAIN), weight_ref[0, MAIN:], preferred_element_type=F32
        )
        product = product.reshape(16, 4, 8, HD)
        for pair in range(4):
            out_ref[pair] = product[:, pair]

    return pl.pallas_call(
        kernel,
        grid=(4,),
        in_specs=[
            pl.BlockSpec((512, MAIN), lambda n: (0, 0)),
            pl.BlockSpec((16, 32, 1024 - MAIN), lambda n: (0, 0, 0)),
            pl.BlockSpec((1, 1024, HD), lambda n: (n, 0, 0)),
        ],
        out_specs=pl.BlockSpec((4, 16, 8, HD), lambda n: (0, 0, 0, n)),
        out_shape=jax.ShapeDtypeStruct((4, 16, 8, 4 * HD), F32),
        compiler_params=pltpu.CompilerParams(vmem_limit_bytes=24 * MIB),
        cost_estimate=cost(2 * 512 * 1024 * 512, 3 * MIB),
    )(main, rest, weights)


def swap_halves(value):
    return pltpu.roll(value, 4, 1)


def query_norm(mine, other, gain):
    def kernel(mine_ref, other_ref, gain_ref, out_ref):
        heads = []
        for h in range(4):
            columns = slice(h * HD, (h + 1) * HD)
            value = mine_ref[:, :, columns] + other_ref[:, :, columns]
            inverse = lax.rsqrt(jnp.mean(value * value, axis=-1, keepdims=True) + EPSILON)
            heads.append(value * inverse * gain_ref[...].reshape(1, 1, HD))
        low = lax.broadcasted_iota(jnp.int32, (16, 8, HD), 1) < 4
        for h in (0, 2):
            rows = slice(h * 4, h * 4 + 8)
            first = jnp.where(low, heads[h], swap_halves(heads[h + 1]))
            second = jnp.where(low, swap_halves(heads[h]), heads[h + 1])
            out_ref[:, 0, rows] = first.astype(BF16)
            out_ref[:, 1, rows] = second.astype(BF16)

    return pl.pallas_call(
        kernel,
        out_shape=jax.ShapeDtypeStruct((16, 2, 16, HD), BF16),
        compiler_params=pltpu.CompilerParams(vmem_limit_bytes=16 * MIB),
        cost_estimate=cost(1 << 20, MIB),
    )(mine, other, gain)


def attend(place, slots, counts, marks, query, keys, values):
    def kernel(place_ref, slots_ref, counts_ref, marks_ref, query_ref, key_ref, value_ref, out_ref):
        slot = place_ref[0] * 2 + pl.program_id(0)
        sequence, image, used = jnp.int32(0), jnp.int32(0), jnp.int32(0)
        for s in range(8):
            for k in range(2):
                hit = jnp.logical_and(slots_ref[s, k] == slot, k < counts_ref[s])
                sequence = jnp.where(hit, s, sequence)
                image = jnp.where(hit, k, image)
                used = jnp.where(hit, 1, used)

        @pl.when(used == 1)
        def _():
            step = lax.broadcasted_iota(jnp.int32, (8, BLOCK_TOK), 0) % STEPS
            lane = lax.broadcasted_iota(jnp.int32, (8, HD), 1)
            blocks = []
            for b in range(IMG_BLK):
                block = jnp.zeros((8, BLOCK_TOK), jnp.int32)
                for t in range(STEPS):
                    block = jnp.where(step == t, marks_ref[sequence * STEPS + t, image * IMG_BLK + b], block)
                blocks.append(block)
            visible = (jnp.concatenate(blocks, axis=1) == 1).reshape(1, 8, IMG_TOK)
            pair, half = sequence // 2, sequence % 2
            for head in range(KVH):
                columns = slice(head * HD, (head + 1) * HD)
                rows = jnp.concatenate([query_ref[pair, 2 * head, half], query_ref[pair, 2 * head + 1, half]], axis=0)
                scores = lax.dot_general(
                    rows, key_ref[:, columns], (((1,), (1,)), ((), ())), preferred_element_type=F32
                ) * HD ** (-0.5)
                scores = scores.reshape(4, 8, IMG_TOK)
                peak = jnp.max(jnp.where(visible, scores, NEGATIVE), axis=-1, keepdims=True)
                expo = jnp.where(visible, jnp.exp(scores - peak), 0.0)
                total = jnp.sum(expo, axis=-1, keepdims=True)
                out_ref[head, 0, :32] = jnp.dot(
                    expo.astype(BF16).reshape(32, IMG_TOK), value_ref[:, columns], preferred_element_type=F32
                )
                figures = jnp.zeros((8, HD), F32)
                for g in range(4):
                    figures = jnp.where(lane == 2 * g, peak[g], figures)
                    figures = jnp.where(lane == 2 * g + 1, total[g], figures)
                out_ref[head, 0, 32:] = figures

    return pl.pallas_call(
        kernel,
        grid=(2,),
        in_specs=[
            SMEM,
            SMEM,
            SMEM,
            SMEM,
            pl.BlockSpec((4, 16, 2, 16, HD), lambda n: (0, 0, 0, 0, 0)),
            pl.BlockSpec((IMG_TOK, KVH * HD), lambda n: (n, 0)),
            pl.BlockSpec((IMG_TOK, KVH * HD), lambda n: (n, 0)),
        ],
        out_specs=pl.BlockSpec((KVH, 1, 40, HD), lambda n: (0, n, 0, 0)),
        out_shape=jax.ShapeDtypeStruct((KVH, 2, 40, HD), F32),
        compiler_params=pltpu.CompilerParams(vmem_limit_bytes=24 * MIB),
        cost_estimate=cost(4 * 2 * 32 * 8 * 512 * 128, 5 * MIB, 2 * 8 * 32 * 512),
    )(place, slots, counts, marks, query, keys, values)


def merge(slots, counts, pieces):
    def kernel(slots_ref, counts_ref, piece_ref, out_ref):
        low = lax.broadcasted_iota(jnp.int32, (8, HD), 0) < 4
        results = []
        for s in range(8):
            first = jnp.clip(slots_ref[s, 0], 0, 15)
            second = jnp.clip(slots_ref[s, 1], 0, 15)
            both = counts_ref[s] > 1
            result = []
            for g in range(4):
                rows = slice(8 * g, 8 * g + 8)
                peak_first = piece_ref[first, 32:, 2 * g : 2 * g + 1]
                total_first = piece_ref[first, 32:, 2 * g + 1 : 2 * g + 2]
                peak_second = jnp.where(both, piece_ref[second, 32:, 2 * g : 2 * g + 1], NEGATIVE)
                total_second = jnp.where(both, piece_ref[second, 32:, 2 * g + 1 : 2 * g + 2], 0.0)
                weighted_second = jnp.where(both, piece_ref[second, rows], 0.0)
                peak = jnp.maximum(peak_first, peak_second)
                factor_first = jnp.exp(peak_first - peak)
                factor_second = jnp.exp(peak_second - peak)
                total = total_first * factor_first + total_second * factor_second
                result.append((piece_ref[first, rows] * factor_first + weighted_second * factor_second) / total)
            results.append(result)
        for h in range(8):
            tiles = []
            for pair in range(4):
                even, odd = results[2 * pair][h // 2], results[2 * pair + 1][h // 2]
                if h % 2 == 0:
                    tiles.append(jnp.where(low, even, pltpu.roll(odd, 4, 0)))
                else:
                    tiles.append(jnp.where(low, pltpu.roll(even, 4, 0), odd))
            out_ref[:, h * HD : (h + 1) * HD] = jnp.concatenate(tiles, axis=0).astype(BF16)

    return pl.pallas_call(
        kernel,
        in_specs=[SMEM, SMEM, pl.BlockSpec(memory_space=pltpu.VMEM)],
        out_shape=jax.ShapeDtypeStruct((32, KVH * HD), BF16),
        compiler_params=pltpu.CompilerParams(vmem_limit_bytes=16 * MIB),
        cost_estimate=cost(1 << 18, MIB // 2, 2048),
    )(slots, counts, pieces)


def out_product(attended, weights):
    def kernel(attended_ref, weight_ref, out_ref):
        product = jnp.dot(attended_ref[...].reshape(256, 1024), weight_ref[0], preferred_element_type=F32)
        product = product.reshape(4, 2, 32, HD)
        for s in range(2):
            out_ref[0, s] = product[:, s]

    return pl.pallas_call(
        kernel,
        grid=(8,),
        in_specs=[
            pl.BlockSpec((4, 2, 32, 1024), lambda n: (0, 0, 0, 0)),
            pl.BlockSpec((1, 1024, HD), lambda n: (n, 0, 0)),
        ],
        out_specs=pl.BlockSpec((1, 2, 4, 32, HD), lambda n: (n, 0, 0, 0, 0)),
        out_shape=jax.ShapeDtypeStruct((8, 2, 4, 32, HD), F32),
        compiler_params=pltpu.CompilerParams(vmem_limit_bytes=24 * MIB),
        cost_estimate=cost(2 * 256 * 1024 * 1024, 4 * MIB),
    )(attended, weights)


def on_device(
    tokens,
    norm_gain,
    w_query,
    query_gain,
    key_cache,
    value_cache,
    block_mask,
    image_counts,
    image_slot,
    attn_gate,
    w_out,
):
    core = lax.axis_index("c")
    place = (lax.axis_index("x") * 2 + core).reshape(1)
    swap = [(0, 1), (1, 0)]

    query_weights = lax.all_gather(w_query, "y")
    query_weights, w_out = lax.optimization_barrier((query_weights, w_out))
    out_weights = lax.all_gather(w_out, "j")

    scaled = (tokens.astype(F32) * norm_gain).astype(BF16)
    rest = jnp.broadcast_to(scaled[None, :, MAIN:], (16, 32, 1024 - MAIN))
    rest = lax.all_to_all(rest, ZED, 0, 0, tiled=True)
    main = lax.all_gather(scaled[:, :MAIN], ZED, axis=0, tiled=True)

    partial = query_product(main, rest, query_weights)
    partial = jnp.sum(lax.all_to_all(partial, "x", 0, 0, tiled=True).reshape(4, 16, 8, 512), axis=0)
    query = query_norm(partial, lax.ppermute(partial, "c", swap), query_gain.reshape(1, HD))
    query = lax.all_to_all(query, ZED, 0, 0, tiled=True)
    query = lax.all_gather(query, "x")

    pieces = attend(place, image_slot, image_counts, block_mask, query, key_cache[0], value_cache[0])
    pieces = lax.all_to_all(pieces, IMG, 0, 0, tiled=True).reshape(16, 40, HD)
    attended = merge(image_slot, image_counts, pieces)

    attended = lax.all_gather(lax.all_gather(attended, "s"), "y")
    partial = out_product(attended, out_weights).reshape(4, 2, 256, HD)
    partial = lax.all_to_all(partial, "x", 0, 0, tiled=True).reshape(4, 2, 256, HD)
    other = jnp.sum(lax.dynamic_index_in_dim(partial, 1 - core, 1, keepdims=False), axis=0)
    other = lax.ppermute(other, "c", swap)
    own = jnp.sum(lax.dynamic_index_in_dim(partial, core, 1, keepdims=False), axis=0)
    mixed = (jnp.tanh(attn_gate[0]) * (own + other)).astype(BF16)
    turn = [(a * 8 + b, b * 8 + a) for a in range(8) for b in range(8)]
    return lax.ppermute(mixed, ("j",) + IMG, turn)


def solution(mesh):
    fine = Mesh(mesh.devices.reshape(SIZES), AXES)
    placed = (
        P(FSDP, IMG),
        P(IMG),
        P(IMG, FSDP),
        P(),
        P(FSDP, IMG, None),
        P(FSDP, IMG, None),
        P(FSDP, None),
        P(FSDP),
        P(FSDP, None),
        P(),
        P(IMG, FSDP),
    )
    return jax.shard_map(on_device, mesh=fine, in_specs=placed, out_specs=P(IMG, FSDP), check_vma=False)
```

time: 565 us -> 264 us (0.47)
  the two profiles are of different devices: /device:TPU:1 before, /device:TPU:2 now
where the time goes in v1:
time: 264 us; the launch traced here: 263 us
  blocking collectives  121 us (46%)
  waiting for transfers between devices  79 us (30%)
  starting transfers between devices  32.6 us (12%)
  between operations  14.2 us (5%)
  Pallas kernels  10.8 us (4%)
  local copies, waits for them, and re-layouts  4.69 us (2%)
    all_gather x1, blocking collectives, on_device(): main = lax.all_gather(scaled[:, :MAIN], ZED, axis=0, tiled=True)  62.8 us
    all_gather x1, waiting for transfers between devices, on_device(): query_weights = lax.all_gather(w_query, 'y')  38.3 us
    all_gather x2, blocking collectives, on_device(): attended = lax.all_gather(lax.all_gather(attended, 's'), 'y')  18.4 us
    all_to_all x1, waiting for transfers between devices, on_device(): query = lax.all_to_all(query, ZED, 0, 0, tiled=True)  14.5 us
    all_to_all x1, blocking collectives, on_device(): lax.all_to_all(partial, 'x', 0, 0, tiled=True).reshape(4, 16, 8, 512)  14.1 us
    all_to_all x1, blocking collectives, on_device(): pieces = lax.all_to_all(pieces, IMG, 0, 0, tiled=True).reshape(16, 40, HD)  13.3 us
    ppermute x1, waiting for transfers between devices, on_device(): return lax.ppermute(mixed, ('j',) + IMG, turn)  12.7 us
    all_to_all x1, starting transfers between devices, on_device(): rest = lax.all_to_all(rest, ZED, 0, 0, tiled=True)  12.3 us
  transfers between devices with their start and end apart: 8, of which 6 were waited for; matrix products, arithmetic and copies ran while one was open for 1% of the time, Pallas kernels for 3%

profile of v1, /device:TPU:2, one launch (start us, length us, event | category | flops | bytes accessed | tf_op | source)
XLA Modules:
  0.0 263.2 jit_solution(1205169528652979322)
XLA Ops:
  6.5 0.0 all-gather.8.cloned.1.call-start
  6.5 0.7 all-gather.8.cloned.1.call-update
  7.3 0.0 all-gather.10.cloned.1.call-start
  7.3 38.3 %all-gather.8.cloned.1.call-done = bf16[4096,128]{1,0:T(8,128)(2,1)} async-done(((bf16[1024,128]{1,0:T(8,128)(2,1)}), bf16[4096,128]{1,0:T(8,128)(2,1)}) %all-gather.8.cloned.1.call-update) | async-done | bytes 1048592 | tf_op jit(solution)/shard_map/all_gather | solution.py:233
  45.6 0.0 copy-start.3
  45.6 0.0 all-gather.10.cloned.1.call-update
  45.6 0.9 multiply_convert_fusion.1
  46.6 0.7 broadcast_in_dim.2
  47.3 12.3 %all-to-all-start = ((bf16[16,32,128]{2,1,0:T(8,128)(2,1)}), bf16[16,32,128]{2,1,0:T(8,128)(2,1)S(1)}, u32[]{:S(2)}, u32[]{:S(2)}) async-start(bf16[16,32,128]{2,1,0:T(8,128)(2,1)} %broadcast_in_dim.2), calls=%async_computation | async-start | bytes 262144 | tf_op jit(solution)/shard_map/all_to_all | solution.py:239
  59.6 62.8 %all_gather.33.main_ref = bf16[512,896]{1,0:T(8,128)(2,1)S(1)} all-gather(bf16[32,896]{1,0:T(8,128)(2,1)S(1)} %slice.8), channel_id=1, replica_groups=mesh['j'=8,'s'=2,'y'=4,'x'=4,'c'=2] {'j','s'}, dimensions={0}, use_global_device_ids=true | all-gather | bytes 974848 | tf_op jit(solution)/shard_map/all_gather | solution.py:240
  122.4 0.0 all-to-all-done.rest_ref
  122.4 0.0 copy-done.3
  122.4 1.8 shard_map.109
  124.2 0.0 copy-start.5
  124.2 0.0 copy-start.7
  124.3 0.0 copy-start.6
  124.3 0.0 copy-start.1
  124.3 0.0 copy-start.4
  124.3 14.1 %all_to_all.25 = f32[4,16,8,512]{3,2,1,0:T(8,128)S(1)} all-to-all(f32[4,16,8,512]{3,2,1,0:T(8,128)S(1)} %shard_map.109), channel_id=1, replica_groups=mesh['j'=8,'s'=2,'y'=4,'x'=4,'c'=2] {'x'}, dimensions={0} | all-to-all | bytes 2097152 | tf_op jit(solution)/shard_map/all_to_all | solution.py:243
  138.4 0.1 reduce_sum.27.mine_ref
  138.5 1.9 collective-permute-start
  140.4 1.5 collective-permute-done.other_ref
  141.9 0.0 copy-done.5
  141.9 0.8 shard_map.110
  142.7 6.1 %all-to-all-start.2 = ((bf16[16,2,16,128]{3,2,1,0:T(8,128)(2,1)}), bf16[16,2,16,128]{3,2,1,0:T(8,128)(2,1)S(1)}, u32[]{:S(2)}, u32[]{:S(2)}) async-start(bf16[16,2,16,128]{3,2,1,0:T(8,128)(2,1)} %shard_map.110), calls=%async_computation.2 | async-start | bytes 262144 | tf_op jit(solution)/shard_map/all_to_all | solution.py:245
  148.8 0.0 copy-done.7
  148.8 0.1 copy.17.slots_ref
  148.9 0.0 copy-done.6
  148.9 0.1 copy.16.marks_ref
  149.0 14.5 %all-to-all-done.2 = bf16[16,2,16,128]{3,2,1,0:T(8,128)(2,1)S(1)} async-done(((bf16[16,2,16,128]{3,2,1,0:T(8,128)(2,1)}), bf16[16,2,16,128]{3,2,1,0:T(8,128)(2,1)S(1)}, u32[]{:S(2)}, u32[]{:S(2)}) %all-to-all-start.2) | async-done | bytes 131104 | tf_op jit(solution)/shard_map/all_to_all | solution.py:245
  163.5 12.2 %all-gather.1 = bf16[64,2,16,128]{3,2,1,0:T(8,128)(2,1)S(1)} all-gather(bf16[16,2,16,128]{3,2,1,0:T(8,128)(2,1)S(1)} %all-to-all-done.2), channel_id=3, replica_groups=mesh['j'=8,'s'=2,'y'=4,'x'=4,'c'=2] {'x'}, dimensions={0}, use_global_device_ids=true | all-gather | bytes 655360 | tf_op jit(solution)/shard_map/all_gather | solution.py:246
  175.7 0.0 copy-done.1
  175.7 0.0 copy-done.4
  175.7 1.6 copy-done.2
  177.3 3.1 %shard_map.111 = f32[8,2,40,128]{3,2,1,0:T(8,128)S(1)} custom-call(s32[1]{0:T(128)} %bitcast.1.place_ref, s32[8,2]{1,0:T(8,128)S(1)} %copy.17.slots_ref, s32[8]{0:T(128)S(1)} %copy-done.4, s32[32,8]{1,0:T(8,128)S(1)} %copy.16.marks_ref, bf16[4,16,2,16,128]{4,3,2,1,0:T(8,128)(2,1)S(1)} %bitcast.13, bf16[1024,1024]{1,0:T(8,128)(2,1)S(1)} %bitcast.15, ...), custom_call_target="tpu_custom_call" | custom-call | flops 134217728 | bytes 5242880 | tf_op jit(solution)/shard_map/pallas_call | solution.py:135
  180.5 13.3 %all_to_all.26 = f32[8,2,40,128]{3,2,1,0:T(8,128)S(1)} all-to-all(f32[8,2,40,128]{3,2,1,0:T(8,128)S(1)} %shard_map.111), channel_id=1, replica_groups=mesh['j'=8,'s'=2,'y'=4,'x'=4,'c'=2] {'x','c'}, dimensions={0} | all-to-all | bytes 655360 | tf_op jit(solution)/shard_map/all_to_all | solution.py:249
  193.8 1.0 shard_map.112
  194.8 4.9 %all-gather.2 = bf16[64,1024]{1,0:T(8,128)(2,1)S(1)} all-gather(bf16[32,1024]{1,0:T(8,128)(2,1)S(1)} %shard_map.112), channel_id=4, replica_groups=mesh['j'=8,'s'=2,'y'=4,'x'=4,'c'=2] {'s'}, dimensions={0}, use_global_device_ids=true | all-gather | bytes 196608 | tf_op jit(solution)/shard_map/all_gather | solution.py:252
  199.7 13.5 %all-gather.3 = bf16[8,32,1024]{2,1,0:T(8,128)(2,1)S(1)} all-gather(bf16[2,32,1024]{2,1,0:T(8,128)(2,1)S(1)} %bitcast.20), channel_id=5, replica_groups=mesh['j'=8,'s'=2,'y'=4,'x'=4,'c'=2] {'y'}, dimensions={0}, use_global_device_ids=true | all-gather | bytes 655360 | tf_op jit(solution)/shard_map/all_gather | solution.py:252
  213.2 1.6 copy-done
  214.8 4.1 %shard_map.113 = f32[8,2,4,32,128]{4,3,2,1,0:T(8,128)} custom-call(bf16[4,2,32,1024]{3,2,1,0:T(8,128)(2,1)S(1)} %bitcast.12, bf16[8,1024,128]{2,1,0:T(8,128)(2,1)S(1)} %bitcast.14), custom_call_target="tpu_custom_call" | custom-call | flops 536870912 | bytes 4194304 | tf_op jit(solution)/shard_map/pallas_call | solution.py:202
  218.8 4.9 %all-to-all-start.4 = ((f32[4,2,256,128]{3,2,1,0:T(8,128)}), f32[4,2,256,128]{3,2,1,0:T(8,128)S(1)}, u32[]{:S(2)}, u32[]{:S(2)}) async-start(f32[4,2,256,128]{3,2,1,0:T(8,128)} %bitcast.11), calls=%async_computation.4 | async-start | bytes 2097152 | tf_op jit(solution)/shard_map/all_to_all | solution.py:254
  223.8 10.5 %all-to-all-done.4 = f32[4,2,256,128]{3,2,1,0:T(8,128)S(1)} async-done(((f32[4,2,256,128]{3,2,1,0:T(8,128)}), f32[4,2,256,128]{3,2,1,0:T(8,128)S(1)}, u32[]{:S(2)}, u32[]{:S(2)}) %all-to-all-start.4) | async-done | bytes 1048608 | tf_op jit(solution)/shard_map/all_to_all | solution.py:254
  234.3 1.9 collective-permute-start.1
  237.0 0.6 collective-permute-done.1
  237.6 5.4 %collective-permute-start.2 = (bf16[256,128]{1,0:T(8,128)(2,1)S(1)}, bf16[256,128]{1,0:T(8,128)(2,1)S(1)}, u32[]{:S(2)}, u32[]{:S(2)}) collective-permute-start(bf16[256,128]{1,0:T(8,128)(2,1)S(1)} %multiply_convert_fusion), channel_id=1, source_target_pairs={{0,0},{1,64},{2,128},{3,192},{4,256},{5,320},{6,384},{7,448},{64,1... | collective-permute-start | bytes 196616 | tf_op jit(solution)/shard_map/ppermute | solution.py:260
  243.0 12.7 %collective-permute-done.2 = bf16[256,128]{1,0:T(8,128)(2,1)S(1)} collective-permute-done((bf16[256,128]{1,0:T(8,128)(2,1)S(1)}, bf16[256,128]{1,0:T(8,128)(2,1)S(1)}, u32[]{:S(2)}, u32[]{:S(2)}) %collective-permute-start.2) | collective-permute-done | bytes 65568 | tf_op jit(solution)/shard_map/ppermute | solution.py:260
  255.8 0.6 copy.20
  (7 shorter events, 0.1 us)
Async XLA Ops:
  6.5 39.1 %all-gather.8.cloned.1.call-start = ((), (), s32[]{:S(2)}) async-start(), calls=%async_computation.5 | async-start | bytes 1310720 | tf_op jit(solution)/shard_map/all_gather | solution.py:233
  7.3 205.9 %all-gather.10.cloned.1.call-start = ((), (), s32[]{:S(2)}) async-start(), calls=%async_computation.6 | async-start | bytes 2359296 | tf_op jit(solution)/shard_map/all_gather | solution.py:235
  45.6 76.8 %copy-start.3 = (bf16[4096,128]{1,0:T(8,128)(2,1)S(1)}, bf16[4096,128]{1,0:T(8,128)(2,1)}, u32[]{:S(2)}) copy-start(bf16[4096,128]{1,0:T(8,128)(2,1)} %all-gather.8.cloned.1.call-done) | copy-start | bytes 3145732
  47.3 75.1 %all-to-all-start = ((bf16[16,32,128]{2,1,0:T(8,128)(2,1)}), bf16[16,32,128]{2,1,0:T(8,128)(2,1)S(1)}, u32[]{:S(2)}, u32[]{:S(2)}) async-start(bf16[16,32,128]{2,1,0:T(8,128)(2,1)} %broadcast_in_dim.2), calls=%async_computation | async-start | bytes 262144 | tf_op jit(solution)/shard_map/all_to_all | solution.py:239
  124.2 17.7 %copy-start.5 = (f32[128]{0:T(128)S(1)}, f32[128]{0:T(128)}, u32[]{:S(2)}) copy-start(f32[128]{0:T(128)} %param.14) | copy-start | bytes 1540
  124.2 24.6 %copy-start.7 = (s32[8,2]{0,1:T(2,128)S(1)}, s32[8,2]{0,1:T(2,128)}, u32[]{:S(2)}) copy-start(s32[8,2]{0,1:T(2,128)} %param.19) | copy-start | bytes 196
  124.3 24.6 %copy-start.6 = (s32[32,8]{0,1:T(8,128)S(1)}, s32[32,8]{0,1:T(8,128)}, u32[]{:S(2)}) copy-start(s32[32,8]{0,1:T(8,128)} %param.17) | copy-start | bytes 3076
  124.3 51.4 %copy-start.1 = (bf16[1,1024,1024]{2,1,0:T(8,128)(2,1)S(1)}, bf16[1,1024,1024]{2,1,0:T(8,128)(2,1)}, u32[]{:S(2)}) copy-start(bf16[1,1024,1024]{2,1,0:T(8,128)(2,1)} %param.15) | copy-start | bytes 6291460
  124.3 51.4 %copy-start.4 = (s32[8]{0:T(128)S(1)}, s32[8]{0:T(128)}, u32[]{:S(2)}) copy-start(s32[8]{0:T(128)} %counts_ref.3) | copy-start | bytes 100
  138.5 3.4 %collective-permute-start = (f32[16,8,512]{2,1,0:T(8,128)S(1)}, f32[16,8,512]{2,1,0:T(8,128)S(1)}, u32[]{:S(2)}, u32[]{:S(2)}) collective-permute-start(f32[16,8,512]{2,1,0:T(8,128)S(1)} %reduce_sum.27.mine_ref), channel_id=1, source_target_pairs={{0,1},{1,0},{2,3},{3,2},{4,5},{5,4},{6,7},{7,6},{8,9},{9,8},{10,11... | collective-permute-start | bytes 786440 | tf_op jit(solution)/shard_map/ppermute | solution.py:244
  142.7 20.8 %all-to-all-start.2 = ((bf16[16,2,16,128]{3,2,1,0:T(8,128)(2,1)}), bf16[16,2,16,128]{3,2,1,0:T(8,128)(2,1)S(1)}, u32[]{:S(2)}, u32[]{:S(2)}) async-start(bf16[16,2,16,128]{3,2,1,0:T(8,128)(2,1)} %shard_map.110), calls=%async_computation.2 | async-start | bytes 262144 | tf_op jit(solution)/shard_map/all_to_all | solution.py:245
  175.7 1.6 copy-start.2
  213.2 1.6 copy-start
  218.8 15.4 %all-to-all-start.4 = ((f32[4,2,256,128]{3,2,1,0:T(8,128)}), f32[4,2,256,128]{3,2,1,0:T(8,128)S(1)}, u32[]{:S(2)}, u32[]{:S(2)}) async-start(f32[4,2,256,128]{3,2,1,0:T(8,128)} %bitcast.11), calls=%async_computation.4 | async-start | bytes 2097152 | tf_op jit(solution)/shard_map/all_to_all | solution.py:254
  234.3 3.2 %collective-permute-start.1 = (f32[256,128]{1,0:T(8,128)S(1)}, f32[256,128]{1,0:T(8,128)S(1)}, u32[]{:S(2)}, u32[]{:S(2)}) collective-permute-start(f32[256,128]{1,0:T(8,128)S(1)} %get-tuple-element.9), channel_id=1, source_target_pairs={{0,1},{1,0},{2,3},{3,2},{4,5},{5,4},{6,7},{7,6},{8,9},{9,8},{10,11... | collective-permute-start | bytes 393224 | tf_op jit(solution)/shard_map/ppermute | solution.py:256
  237.6 18.2 %collective-permute-start.2 = (bf16[256,128]{1,0:T(8,128)(2,1)S(1)}, bf16[256,128]{1,0:T(8,128)(2,1)S(1)}, u32[]{:S(2)}, u32[]{:S(2)}) collective-permute-start(bf16[256,128]{1,0:T(8,128)(2,1)S(1)} %multiply_convert_fusion), channel_id=1, source_target_pairs={{0,0},{1,64},{2,128},{3,192},{4,256},{5,320},{6,384},{7,448},{64,1... | collective-permute-start | bytes 196616 | tf_op jit(solution)/shard_map/ppermute | solution.py:260
Sparse Core Ops, SparseCore 0:
  9.5 36.1 all-gather.7
  47.7 71.2 all-gather.9

commit v2 on v1

--- a/solution.py
+++ b/solution.py
@@ -39,23 +39,22 @@
 
 def query_product(main, rest, weights):
     def kernel(main_ref, rest_ref, weight_ref, out_ref):
-        product = jnp.dot(main_ref[...], weight_ref[0, :MAIN], preferred_element_type=F32)
-        product += jnp.dot(
-            rest_ref[...].reshape(512, 1024 - MAIN), weight_ref[0, MAIN:], preferred_element_type=F32
-        )
-        product = product.reshape(16, 4, 8, HD)
+        weight = jnp.concatenate([weight_ref[0], weight_ref[1]], axis=1)
+        product = jnp.dot(main_ref[...], weight[:MAIN], preferred_element_type=F32)
+        product += jnp.dot(rest_ref[...].reshape(512, 1024 - MAIN), weight[MAIN:], preferred_element_type=F32)
+        product = product.reshape(16, 4, 8, 2 * HD)
         for pair in range(4):
             out_ref[pair] = product[:, pair]
 
     return pl.pallas_call(
         kernel,
-        grid=(4,),
+        grid=(2,),
         in_specs=[
             pl.BlockSpec((512, MAIN), lambda n: (0, 0)),
             pl.BlockSpec((16, 32, 1024 - MAIN), lambda n: (0, 0, 0)),
-            pl.BlockSpec((1, 1024, HD), lambda n: (n, 0, 0)),
+            pl.BlockSpec((2, 1024, HD), lambda n: (n, 0, 0)),
         ],
-        out_specs=pl.BlockSpec((4, 16, 8, HD), lambda n: (0, 0, 0, n)),
+        out_specs=pl.BlockSpec((4, 16, 8, 2 * HD), lambda n: (0, 0, 0, n)),
         out_shape=jax.ShapeDtypeStruct((4, 16, 8, 4 * HD), F32),
         compiler_params=pltpu.CompilerParams(vmem_limit_bytes=24 * MIB),
         cost_estimate=cost(2 * 512 * 1024 * 512, 3 * MIB),
@@ -181,12 +180,14 @@
                     tiles.append(jnp.where(low, even, pltpu.roll(odd, 4, 0)))
                 else:
                     tiles.append(jnp.where(low, pltpu.roll(even, 4, 0), odd))
-            out_ref[:, h * HD : (h + 1) * HD] = jnp.concatenate(tiles, axis=0).astype(BF16)
+            tile = jnp.concatenate(tiles, axis=0).astype(BF16)
+            for copy in range(8):
+                out_ref[copy, :, h * HD : (h + 1) * HD] = tile
 
     return pl.pallas_call(
         kernel,
         in_specs=[SMEM, SMEM, pl.BlockSpec(memory_space=pltpu.VMEM)],
-        out_shape=jax.ShapeDtypeStruct((32, KVH * HD), BF16),
+        out_shape=jax.ShapeDtypeStruct((8, 32, KVH * HD), BF16),
         compiler_params=pltpu.CompilerParams(vmem_limit_bytes=16 * MIB),
         cost_estimate=cost(1 << 18, MIB // 2, 2048),
     )(slots, counts, pieces)
@@ -194,20 +195,20 @@
 
 def out_product(attended, weights):
     def kernel(attended_ref, weight_ref, out_ref):
-        product = jnp.dot(attended_ref[...].reshape(256, 1024), weight_ref[0], preferred_element_type=F32)
-        product = product.reshape(4, 2, 32, HD)
-        for s in range(2):
-            out_ref[0, s] = product[:, s]
-
-    return pl.pallas_call(
-        kernel,
-        grid=(8,),
+        weight = jnp.concatenate([weight_ref[0], weight_ref[1]], axis=1)
+        product = jnp.dot(attended_ref[...], weight, preferred_element_type=F32)
+        out_ref[0] = product[:, :HD]
+        out_ref[1] = product[:, HD:]
+
+    return pl.pallas_call(
+        kernel,
+        grid=(4,),
         in_specs=[
-            pl.BlockSpec((4, 2, 32, 1024), lambda n: (0, 0, 0, 0)),
-            pl.BlockSpec((1, 1024, HD), lambda n: (n, 0, 0)),
+            pl.BlockSpec((256, 1024), lambda n: (0, 0)),
+            pl.BlockSpec((2, 1024, HD), lambda n: (n, 0, 0)),
         ],
-        out_specs=pl.BlockSpec((1, 2, 4, 32, HD), lambda n: (n, 0, 0, 0, 0)),
-        out_shape=jax.ShapeDtypeStruct((8, 2, 4, 32, HD), F32),
+        out_specs=pl.BlockSpec((2, 256, HD), lambda n: (n, 0, 0)),
+        out_shape=jax.ShapeDtypeStruct((8, 256, HD), F32),
         compiler_params=pltpu.CompilerParams(vmem_limit_bytes=24 * MIB),
         cost_estimate=cost(2 * 256 * 1024 * 1024, 4 * MIB),
     )(attended, weights)
@@ -231,25 +232,24 @@
     swap = [(0, 1), (1, 0)]
 
     query_weights = lax.all_gather(w_query, "y")
-    query_weights, w_out = lax.optimization_barrier((query_weights, w_out))
-    out_weights = lax.all_gather(w_out, "j")
-
     scaled = (tokens.astype(F32) * norm_gain).astype(BF16)
     rest = jnp.broadcast_to(scaled[None, :, MAIN:], (16, 32, 1024 - MAIN))
     rest = lax.all_to_all(rest, ZED, 0, 0, tiled=True)
     main = lax.all_gather(scaled[:, :MAIN], ZED, axis=0, tiled=True)
+    main, w_out = lax.optimization_barrier((main, w_out))
+    out_weights = lax.all_gather(w_out, "j")
 
     partial = query_product(main, rest, query_weights)
     partial = jnp.sum(lax.all_to_all(partial, "x", 0, 0, tiled=True).reshape(4, 16, 8, 512), axis=0)
     query = query_norm(partial, lax.ppermute(partial, "c", swap), query_gain.reshape(1, HD))
     query = lax.all_to_all(query, ZED, 0, 0, tiled=True)
-    query = lax.all_gather(query, "x")
+    query = lax.all_to_all(jnp.broadcast_to(query, (4, 16, 2, 16, HD)), "x", 0, 0, tiled=True)
 
     pieces = attend(place, image_slot, image_counts, block_mask, query, key_cache[0], value_cache[0])
     pieces = lax.all_to_all(pieces, IMG, 0, 0, tiled=True).reshape(16, 40, HD)
     attended = merge(image_slot, image_counts, pieces)
 
-    attended = lax.all_gather(lax.all_gather(attended, "s"), "y")
+    attended = lax.all_to_all(attended, ("s", "y"), 0, 0, tiled=True).reshape(256, 1024)
     partial = out_product(attended, out_weights).reshape(4, 2, 256, HD)
     partial = lax.all_to_all(partial, "x", 0, 0, tiled=True).reshape(4, 2, 256, HD)
     other = jnp.sum(lax.dynamic_index_in_dim(partial, 1 - core, 1, keepdims=False), axis=0)

time: 264 us -> 210 us (0.80)
  the two profiles are of different devices: /device:TPU:2 before, /device:TPU:44 now
where the time goes in v2:
time: 210 us; the launch traced here: 209 us
  blocking collectives  79.7 us (38%)
  starting transfers between devices  49.3 us (23%)
  waiting for transfers between devices  46.2 us (22%)
  between operations  15.6 us (7%)
  Pallas kernels  9.21 us (4%)
  local copies, waits for them, and re-layouts  6.78 us (3%)
  other arithmetic  2.25 us (1%)
    all_gather x1, blocking collectives, on_device(): main = lax.all_gather(scaled[:, :MAIN], ZED, axis=0, tiled=True)  36.4 us
    all_to_all x1, blocking collectives, on_device(): query = lax.all_to_all(query, ZED, 0, 0, tiled=True)  30.1 us
    all_to_all x1, starting transfers between devices, on_device(): rest = lax.all_to_all(rest, ZED, 0, 0, tiled=True)  15.2 us
    all_to_all x1, blocking collectives, on_device(): pieces = lax.all_to_all(pieces, IMG, 0, 0, tiled=True).reshape(16, 40, HD)  13.2 us
    all_to_all x1, waiting for transfers between devices, on_device(): lax.all_to_all(partial, 'x', 0, 0, tiled=True).reshape(4, 2, 256, HD)  12.6 us
    ppermute x1, waiting for transfers between devices, on_device(): return lax.ppermute(mixed, ('j',) + IMG, turn)  9.07 us
    ppermute x1, starting transfers between devices, on_device(): return lax.ppermute(mixed, ('j',) + IMG, turn)  8.2 us
    all_to_all x1, waiting for transfers between devices, on_device(): lax.all_to_all(attended, ('s', 'y'), 0, 0, tiled=True).reshape(256, 1024)  7.91 us
  transfers between devices with their start and end apart: 10, of which 7 were waited for; matrix products, arithmetic and copies ran while one was open for 2% of the time, Pallas kernels for 2%

profile of v2, /device:TPU:44, one launch (start us, length us, event | category | flops | bytes accessed | tf_op | source)
XLA Modules:
  0.0 209.1 jit_solution(8344287120023614342)
XLA Ops:
  7.4 0.0 all-gather.5.cloned.1.call-start
  7.4 0.7 all-gather.5.cloned.1.call-update
  8.1 0.9 multiply_convert_fusion.1
  9.0 0.7 broadcast_in_dim.4
  9.6 15.2 %all-to-all-start = ((bf16[16,32,128]{2,1,0:T(8,128)(2,1)}), bf16[16,32,128]{2,1,0:T(8,128)(2,1)S(1)}, u32[]{:S(2)}, u32[]{:S(2)}) async-start(bf16[16,32,128]{2,1,0:T(8,128)(2,1)} %broadcast_in_dim.4), calls=%async_computation | async-start | bytes 262144 | tf_op jit(solution)/shard_map/all_to_all | solution.py:237
  24.9 36.4 %all_gather.15.main_ref = bf16[512,896]{1,0:T(8,128)(2,1)S(1)} all-gather(bf16[32,896]{1,0:T(8,128)(2,1)S(1)} %slice.8), channel_id=1, replica_groups=mesh['j'=8,'s'=2,'y'=4,'x'=4,'c'=2] {'j','s'}, dimensions={0}, use_global_device_ids=true | all-gather | bytes 974848 | tf_op jit(solution)/shard_map/all_gather | solution.py:238
  61.3 0.0 all-to-all-done.rest_ref
  61.3 0.0 all-gather.5.cloned.1.call-done
  61.3 0.0 copy-start.3
  61.3 1.2 copy-done.3
  62.5 1.8 shard_map.109
  64.3 0.0 copy-start.5
  64.3 4.9 %all-to-all-start.1 = ((f32[4,16,8,512]{3,2,1,0:T(8,128)}), f32[4,16,8,512]{3,2,1,0:T(8,128)}, u32[]{:S(2)}, u32[]{:S(2)}) async-start(f32[4,16,8,512]{3,2,1,0:T(8,128)} %shard_map.109), calls=%async_computation.1 | async-start | bytes 2097152 | tf_op jit(solution)/shard_map/all_to_all | solution.py:243
  69.2 0.0 copy-start.7
  69.2 0.0 copy-start.6
  69.2 0.0 all-gather.7.cloned.1.call-start
  69.3 0.5 all-gather.7.cloned.1.call-update
  69.8 7.4 %all-to-all-done.1 = f32[4,16,8,512]{3,2,1,0:T(8,128)} async-done(((f32[4,16,8,512]{3,2,1,0:T(8,128)}), f32[4,16,8,512]{3,2,1,0:T(8,128)}, u32[]{:S(2)}, u32[]{:S(2)}) %all-to-all-start.1) | async-done | bytes 1048608 | tf_op jit(solution)/shard_map/all_to_all | solution.py:243
  77.3 1.3 reduce_sum.27.mine_ref
  78.6 1.9 collective-permute-start
  80.5 1.5 collective-permute-done.other_ref
  82.0 0.0 copy-done.5
  82.0 0.2 shard_map.110
  82.2 30.1 %all_to_all.35 = bf16[16,2,16,128]{3,2,1,0:T(8,128)(2,1)S(1)} all-to-all(bf16[16,2,16,128]{3,2,1,0:T(8,128)(2,1)S(1)} %shard_map.110), channel_id=1, replica_groups=mesh['j'=8,'s'=2,'y'=4,'x'=4,'c'=2] {'j','s'}, dimensions={0} | all-to-all | bytes 262144 | tf_op jit(solution)/shard_map/all_to_all | solution.py:245
  112.3 0.9 broadcast_in_dim.5
  113.2 4.8 %all-to-all-start.3 = ((bf16[4,16,2,16,128]{4,3,2,1,0:T(8,128)(2,1)}), bf16[4,16,2,16,128]{4,3,2,1,0:T(8,128)(2,1)S(1)}, u32[]{:S(2)}, u32[]{:S(2)}) async-start(bf16[4,16,2,16,128]{4,3,2,1,0:T(8,128)(2,1)} %broadcast_in_dim.5), calls=%async_computation.3 | async-start | bytes 1048576 | tf_op jit(solution)/shard_map/all_to_all | solution.py:246
  118.0 0.0 copy-done.7
  118.0 0.1 copy.14.slots_ref
  118.1 0.0 copy-done.6
  118.1 0.1 copy.13.marks_ref
  118.2 5.8 %all-to-all-done.3.query_ref = bf16[4,16,2,16,128]{4,3,2,1,0:T(8,128)(2,1)S(1)} async-done(((bf16[4,16,2,16,128]{4,3,2,1,0:T(8,128)(2,1)}), bf16[4,16,2,16,128]{4,3,2,1,0:T(8,128)(2,1)S(1)}, u32[]{:S(2)}, u32[]{:S(2)}) %all-to-all-start.3) | async-done | bytes 524320 | tf_op jit(solution)/shard_map/all_to_all | solution.py:246
  124.0 0.0 copy-done.1
  124.0 0.0 copy-done.4
  124.0 1.6 copy-done.2
  125.6 3.1 %shard_map.111 = f32[8,2,40,128]{3,2,1,0:T(8,128)S(1)} custom-call(s32[1]{0:T(128)} %bitcast.1.place_ref, s32[8,2]{1,0:T(8,128)S(1)} %copy.14.slots_ref, s32[8]{0:T(128)S(1)} %copy-done.4, s32[32,8]{1,0:T(8,128)S(1)} %copy.13.marks_ref, bf16[4,16,2,16,128]{4,3,2,1,0:T(8,128)(2,1)S(1)} %all-to-all-done.3.query_ref, bf16[1024,1024]{1,0:T(8,128)(2,1)S(1)} %bitcast.12, ...), custom_call_target="tpu_custom_call" | custom-call | flops 134217728 | bytes 5242880 | tf_op jit(solution)/shard_map/pallas_call | solution.py:134
  128.8 13.2 %all_to_all.36 = f32[8,2,40,128]{3,2,1,0:T(8,128)S(1)} all-to-all(f32[8,2,40,128]{3,2,1,0:T(8,128)S(1)} %shard_map.111), channel_id=1, replica_groups=mesh['j'=8,'s'=2,'y'=4,'x'=4,'c'=2] {'x','c'}, dimensions={0} | all-to-all | bytes 655360 | tf_op jit(solution)/shard_map/all_to_all | solution.py:249
  141.9 1.8 shard_map.112
  143.7 6.3 %all-to-all-start.5 = ((bf16[8,32,1024]{2,1,0:T(8,128)(2,1)}), bf16[8,32,1024]{2,1,0:T(8,128)(2,1)S(1)}, u32[]{:S(2)}, u32[]{:S(2)}) async-start(bf16[8,32,1024]{2,1,0:T(8,128)(2,1)} %shard_map.112), calls=%async_computation.5 | async-start | bytes 1048576 | tf_op jit(solution)/shard_map/all_to_all | solution.py:252
  149.9 7.9 %all-to-all-done.5 = bf16[8,32,1024]{2,1,0:T(8,128)(2,1)S(1)} async-done(((bf16[8,32,1024]{2,1,0:T(8,128)(2,1)}), bf16[8,32,1024]{2,1,0:T(8,128)(2,1)S(1)}, u32[]{:S(2)}, u32[]{:S(2)}) %all-to-all-start.5) | async-done | bytes 524320 | tf_op jit(solution)/shard_map/all_to_all | solution.py:252
  157.9 1.6 copy-done
  159.5 2.3 %shard_map.113 = f32[8,256,128]{2,1,0:T(8,128)} custom-call(bf16[256,1024]{1,0:T(8,128)(2,1)S(1)} %bitcast.11, bf16[8,1024,128]{2,1,0:T(8,128)(2,1)S(1)} %bitcast.10), custom_call_target="tpu_custom_call" | custom-call | flops 536870912 | bytes 4194304 | tf_op jit(solution)/shard_map/pallas_call | solution.py:203
  161.8 6.0 %all-to-all-start.6 = ((f32[4,2,256,128]{3,2,1,0:T(8,128)}), f32[4,2,256,128]{3,2,1,0:T(8,128)S(1)}, u32[]{:S(2)}, u32[]{:S(2)}) async-start(f32[4,2,256,128]{3,2,1,0:T(8,128)} %bitcast.9), calls=%async_computation.6 | async-start | bytes 2097152 | tf_op jit(solution)/shard_map/all_to_all | solution.py:254
  167.8 12.6 %all-to-all-done.6 = f32[4,2,256,128]{3,2,1,0:T(8,128)S(1)} async-done(((f32[4,2,256,128]{3,2,1,0:T(8,128)}), f32[4,2,256,128]{3,2,1,0:T(8,128)S(1)}, u32[]{:S(2)}, u32[]{:S(2)}) %all-to-all-start.6) | async-done | bytes 1048608 | tf_op jit(solution)/shard_map/all_to_all | solution.py:254
  180.5 1.9 collective-permute-start.1
  183.1 0.6 collective-permute-done.1
  183.7 8.2 %collective-permute-start.2 = (bf16[256,128]{1,0:T(8,128)(2,1)S(1)}, bf16[256,128]{1,0:T(8,128)(2,1)S(1)}, u32[]{:S(2)}, u32[]{:S(2)}) collective-permute-start(bf16[256,128]{1,0:T(8,128)(2,1)S(1)} %multiply_convert_fusion), channel_id=1, source_target_pairs={{0,0},{1,64},{2,128},{3,192},{4,256},{5,320},{6,384},{7,448},{64,1... | collective-permute-start | bytes 196616 | tf_op jit(solution)/shard_map/ppermute | solution.py:260
  191.9 9.1 %collective-permute-done.2 = bf16[256,128]{1,0:T(8,128)(2,1)S(1)} collective-permute-done((bf16[256,128]{1,0:T(8,128)(2,1)S(1)}, bf16[256,128]{1,0:T(8,128)(2,1)S(1)}, u32[]{:S(2)}, u32[]{:S(2)}) %collective-permute-start.2) | collective-permute-done | bytes 65568 | tf_op jit(solution)/shard_map/ppermute | solution.py:260
  201.0 0.6 copy.17
  (9 shorter events, 0.1 us)
Async XLA Ops:
  7.4 53.9 %all-gather.5.cloned.1.call-start = ((), (), s32[]{:S(2)}) async-start(), calls=%async_computation.7 | async-start | bytes 1310720 | tf_op jit(solution)/shard_map/all_gather | solution.py:234
  9.6 51.6 %all-to-all-start = ((bf16[16,32,128]{2,1,0:T(8,128)(2,1)}), bf16[16,32,128]{2,1,0:T(8,128)(2,1)S(1)}, u32[]{:S(2)}, u32[]{:S(2)}) async-start(bf16[16,32,128]{2,1,0:T(8,128)(2,1)} %broadcast_in_dim.4), calls=%async_computation | async-start | bytes 262144 | tf_op jit(solution)/shard_map/all_to_all | solution.py:237
  61.3 1.2 copy-start.3
  64.3 17.7 %copy-start.5 = (f32[128]{0:T(128)S(1)}, f32[128]{0:T(128)}, u32[]{:S(2)}) copy-start(f32[128]{0:T(128)} %param.14) | copy-start | bytes 1540
  64.3 13.0 %all-to-all-start.1 = ((f32[4,16,8,512]{3,2,1,0:T(8,128)}), f32[4,16,8,512]{3,2,1,0:T(8,128)}, u32[]{:S(2)}, u32[]{:S(2)}) async-start(f32[4,16,8,512]{3,2,1,0:T(8,128)} %shard_map.109), calls=%async_computation.1 | async-start | bytes 2097152 | tf_op jit(solution)/shard_map/all_to_all | solution.py:243
  69.2 48.8 %copy-start.7 = (s32[8,2]{0,1:T(2,128)S(1)}, s32[8,2]{0,1:T(2,128)}, u32[]{:S(2)}) copy-start(s32[8,2]{0,1:T(2,128)} %param.19) | copy-start | bytes 196
  69.2 48.8 %copy-start.6 = (s32[32,8]{0,1:T(8,128)S(1)}, s32[32,8]{0,1:T(8,128)}, u32[]{:S(2)}) copy-start(s32[32,8]{0,1:T(8,128)} %param.17) | copy-start | bytes 3076
  69.2 54.8 %copy-start.1 = (bf16[1,1024,1024]{2,1,0:T(8,128)(2,1)S(1)}, bf16[1,1024,1024]{2,1,0:T(8,128)(2,1)}, u32[]{:S(2)}) copy-start(bf16[1,1024,1024]{2,1,0:T(8,128)(2,1)} %param.15) | copy-start | bytes 6291460
  69.2 54.8 %copy-start.4 = (s32[8]{0:T(128)S(1)}, s32[8]{0:T(128)}, u32[]{:S(2)}) copy-start(s32[8]{0:T(128)} %counts_ref.3) | copy-start | bytes 100
  69.2 80.7 %all-gather.7.cloned.1.call-start = ((), (), s32[]{:S(2)}) async-start(), calls=%async_computation.8 | async-start | bytes 2359296 | tf_op jit(solution)/shard_map/all_gather | solution.py:240
  78.6 3.4 %collective-permute-start = (f32[16,8,512]{2,1,0:T(8,128)S(1)}, f32[16,8,512]{2,1,0:T(8,128)S(1)}, u32[]{:S(2)}, u32[]{:S(2)}) collective-permute-start(f32[16,8,512]{2,1,0:T(8,128)S(1)} %reduce_sum.27.mine_ref), channel_id=1, source_target_pairs={{0,1},{1,0},{2,3},{3,2},{4,5},{5,4},{6,7},{7,6},{8,9},{9,8},{10,11... | collective-permute-start | bytes 786440 | tf_op jit(solution)/shard_map/ppermute | solution.py:244
  113.2 10.8 %all-to-all-start.3 = ((bf16[4,16,2,16,128]{4,3,2,1,0:T(8,128)(2,1)}), bf16[4,16,2,16,128]{4,3,2,1,0:T(8,128)(2,1)S(1)}, u32[]{:S(2)}, u32[]{:S(2)}) async-start(bf16[4,16,2,16,128]{4,3,2,1,0:T(8,128)(2,1)} %broadcast_in_dim.5), calls=%async_computation.3 | async-start | bytes 1048576 | tf_op jit(solution)/shard_map/all_to_all | solution.py:246
  124.0 1.6 copy-start.2
  143.7 14.2 %all-to-all-start.5 = ((bf16[8,32,1024]{2,1,0:T(8,128)(2,1)}), bf16[8,32,1024]{2,1,0:T(8,128)(2,1)S(1)}, u32[]{:S(2)}, u32[]{:S(2)}) async-start(bf16[8,32,1024]{2,1,0:T(8,128)(2,1)} %shard_map.112), calls=%async_computation.5 | async-start | bytes 1048576 | tf_op jit(solution)/shard_map/all_to_all | solution.py:252
  157.9 1.6 copy-start
  161.8 18.6 %all-to-all-start.6 = ((f32[4,2,256,128]{3,2,1,0:T(8,128)}), f32[4,2,256,128]{3,2,1,0:T(8,128)S(1)}, u32[]{:S(2)}, u32[]{:S(2)}) async-start(f32[4,2,256,128]{3,2,1,0:T(8,128)} %bitcast.9), calls=%async_computation.6 | async-start | bytes 2097152 | tf_op jit(solution)/shard_map/all_to_all | solution.py:254
  180.5 3.2 %collective-permute-start.1 = (f32[256,128]{1,0:T(8,128)S(1)}, f32[256,128]{1,0:T(8,128)S(1)}, u32[]{:S(2)}, u32[]{:S(2)}) collective-permute-start(f32[256,128]{1,0:T(8,128)S(1)} %get-tuple-element.9), channel_id=1, source_target_pairs={{0,1},{1,0},{2,3},{3,2},{4,5},{5,4},{6,7},{7,6},{8,9},{9,8},{10,11... | collective-permute-start | bytes 393224 | tf_op jit(solution)/shard_map/ppermute | solution.py:256
  183.7 17.3 %collective-permute-start.2 = (bf16[256,128]{1,0:T(8,128)(2,1)S(1)}, bf16[256,128]{1,0:T(8,128)(2,1)S(1)}, u32[]{:S(2)}, u32[]{:S(2)}) collective-permute-start(bf16[256,128]{1,0:T(8,128)(2,1)S(1)} %multiply_convert_fusion), channel_id=1, source_target_pairs={{0,0},{1,64},{2,128},{3,192},{4,256},{5,320},{6,384},{7,448},{64,1... | collective-permute-start | bytes 196616 | tf_op jit(solution)/shard_map/ppermute | solution.py:260
Sparse Core Ops, SparseCore 0:
  10.3 34.3 all-gather.4
Sparse Core Ops, SparseCore 1:
  71.8 68.1 all-gather.6

commit v3 on v0

v3 whole, which is shorter than its diff:
```python
import functools

import jax
import jax.numpy as jnp
from jax import lax
from jax.experimental import pallas as pl
from jax.experimental.pallas import tpu as pltpu
from jax.sharding import Mesh
from jax.sharding import PartitionSpec as P

H = 64
KVH = 8
HD = 128
IMG_BLK = 4
BLOCK_TOK = 128
IMG_TOK = 512
STEPS = 4

NEGATIVE = -1e30
EPSILON = 1e-05

BF16 = jnp.bfloat16
F32 = jnp.float32
MIB = 1 << 20

AXES = ("j", "s", "y", "x", "c")
SIZES = (8, 2, 4, 4, 2)
NEAR = ("s", "y")
IMG = ("x", "c")
FSDP = ("j", "s", "y")

SMEM = pl.BlockSpec(memory_space=pltpu.SMEM)


def cost(flops, size, exps=0):
    return pl.CostEstimate(flops=flops, bytes_accessed=size, transcendentals=exps)


def product(rows, weights, kept):
    def kernel(rows_ref, weight_ref, out_ref):
        weight = jnp.concatenate([weight_ref[0], weight_ref[1]], axis=1)
        total = jnp.dot(rows_ref[...], weight, preferred_element_type=F32)
        out_ref[0] = total[:, :HD].astype(kept)
        out_ref[1] = total[:, HD:].astype(kept)

    return pl.pallas_call(
        kernel,
        grid=(4,),
        in_specs=[
            pl.BlockSpec((256, 1024), lambda n: (0, 0)),
            pl.BlockSpec((2, 1024, HD), lambda n: (n, 0, 0)),
        ],
        out_specs=pl.BlockSpec((2, 256, HD), lambda n: (n, 0, 0)),
        out_shape=jax.ShapeDtypeStruct((8, 256, HD), kept),
        compiler_params=pltpu.CompilerParams(vmem_limit_bytes=24 * MIB),
        cost_estimate=cost(2 * 256 * 1024 * 1024, 4 * MIB),
    )(rows, weights)


def query_norm(parts, gain):
    def kernel(part_ref, gain_ref, out_ref):
        value = jnp.sum(part_ref[...], axis=0)
        inverse = lax.rsqrt(jnp.mean(value * value, axis=-1, keepdims=True) + EPSILON)
        out_ref[...] = (value * inverse * gain_ref[...]).astype(BF16)

    return pl.pallas_call(
        kernel,
        out_shape=jax.ShapeDtypeStruct((256, HD), BF16),
        compiler_params=pltpu.CompilerParams(vmem_limit_bytes=16 * MIB),
        cost_estimate=cost(1 << 18, MIB // 4),
    )(parts, gain)


def attend(slots, counts, marks, query, caches):
    def kernel(slots_ref, counts_ref, marks_ref, query_ref, cache_ref, out_ref):
        step = lax.broadcasted_iota(jnp.int32, (8, BLOCK_TOK), 0) % STEPS
        low = lax.broadcasted_iota(jnp.int32, (8, HD), 0) < 4
        heads = [query_ref[h % 4 * 2 + h // 4].astype(F32) for h in range(8)]
        results = []
        for s in range(8):
            blocks, scores, places = [], [], []
            tiles = []
            for h in range(0, 8, 2):
                even, odd = (head[s // 2 * 8 : s // 2 * 8 + 8] for head in heads[h : h + 2])
                if s % 2 == 0:
                    tiles.append(jnp.where(low, even, pltpu.roll(odd, 4, 0)))
                else:
                    tiles.append(jnp.where(low, pltpu.roll(even, 4, 0), odd))
            rows = jnp.concatenate(tiles, axis=0).astype(BF16)
            for k in range(2):
                slot = jnp.clip(slots_ref[s, k], 0, 15)
                places.append((slot // 2, slot % 2))
                live = (k < counts_ref[s]).astype(jnp.int32)
                for b in range(IMG_BLK):
                    block = jnp.zeros((8, BLOCK_TOK), jnp.int32)
                    for t in range(STEPS):
                        block = jnp.where(step == t, marks_ref[s * STEPS + t, k * IMG_BLK + b] * live, block)
                    blocks.append(block)
                scores.append(
                    lax.dot_general(
                        rows,
                        cache_ref[places[k][0], 0, places[k][1]],
                        (((1,), (1,)), ((), ())),
                        preferred_element_type=F32,
                    )
                )
            visible = (jnp.concatenate(blocks, axis=1) == 1).reshape(1, 8, 2 * IMG_TOK)
            score = (jnp.concatenate(scores, axis=1) * HD ** (-0.5)).reshape(4, 8, 2 * IMG_TOK)
            peak = jnp.max(jnp.where(visible, score, NEGATIVE), axis=-1, keepdims=True)
            expo = jnp.where(visible, jnp.exp(score - peak), 0.0)
            total = jnp.sum(expo, axis=-1, keepdims=True)
            expo = expo.astype(BF16).reshape(32, 2 * IMG_TOK)
            weighted = jnp.dot(
                expo[:, :IMG_TOK], cache_ref[places[0][0], 1, places[0][1]], preferred_element_type=F32
            ) + jnp.dot(expo[:, IMG_TOK:], cache_ref[places[1][0], 1, places[1][1]], preferred_element_type=F32)
            results.append(weighted.reshape(4, 8, HD) / total)
        for h in range(8):
            tiles = []
            for pair in range(4):
                even, odd = results[2 * pair][h // 2], results[2 * pair + 1][h // 2]
                if h % 2 == 0:
                    tiles.append(jnp.where(low, even, pltpu.roll(odd, 4, 0)))
                else:
                    tiles.append(jnp.where(low, pltpu.roll(even, 4, 0), odd))
            tile = jnp.concatenate(tiles, axis=0).astype(BF16)
            out_ref[:, h * HD : (h + 1) * HD] = tile

    whole = pl.BlockSpec(memory_space=pltpu.VMEM)
    return pl.pallas_call(
        kernel,
        in_specs=[SMEM, SMEM, SMEM, whole, whole],
        out_specs=whole,
        out_shape=jax.ShapeDtypeStruct((32, KVH * HD), BF16),
        compiler_params=pltpu.CompilerParams(vmem_limit_bytes=24 * MIB),
        cost_estimate=cost(4 * 2 * 32 * 8 * 512 * 128, 5 * MIB, 2 * 8 * 32 * 512),
    )(slots, counts, marks, query, caches)


def on_device(
    tokens,
    norm_gain,
    w_query,
    query_gain,
    key_cache,
    value_cache,
    block_mask,
    image_counts,
    image_slot,
    attn_gate,
    w_out,
):
    query_weights = lax.all_gather(w_query, "j")
    caches = jnp.stack([key_cache[0], value_cache[0]]).reshape(2, 1024, KVH, HD).transpose(2, 0, 1, 3)
    caches, tokens = lax.optimization_barrier((caches, tokens))
    caches = lax.all_to_all(caches, IMG, 0, 0, tiled=True)
    scaled = (tokens.astype(F32) * norm_gain).astype(BF16)
    scaled = lax.all_gather(lax.all_gather(scaled, "s"), "y")

    partial = product(scaled.reshape(256, 1024), query_weights, F32).reshape(4, 2, 256, HD)
    partial, caches, w_out = lax.optimization_barrier((partial, caches, w_out))
    out_weights = lax.all_gather(w_out, NEAR)
    partial = lax.all_to_all(partial.reshape(8, 256, HD), IMG, 0, 0, tiled=True)
    query = query_norm(partial, query_gain.reshape(1, HD))
    query = lax.all_to_all(query.reshape(8, 32, HD), ("y", "s"), 0, 0, tiled=True)
    attended = attend(image_slot, image_counts, block_mask, query, caches.reshape(8, 2, 2, IMG_TOK, HD))

    attended = lax.all_gather(attended, "j", axis=0, tiled=True)
    partial = product(attended, out_weights, BF16).reshape(64, 32, HD)
    partial = lax.all_to_all(partial, NEAR + IMG, 0, 0, tiled=True).reshape(8, 8, 32, HD)
    return (jnp.tanh(attn_gate[0]) * jnp.sum(partial.astype(F32), axis=1)).astype(BF16).reshape(256, HD)


def solution(mesh):
    fine = Mesh(mesh.devices.reshape(SIZES), AXES)
    placed = (
        P(FSDP, IMG),
        P(IMG),
        P(IMG, FSDP),
        P(),
        P(FSDP, IMG, None),
        P(FSDP, IMG, None),
        P(FSDP, None),
        P(FSDP),
        P(FSDP, None),
        P(),
        P(IMG, FSDP),
    )
    return jax.shard_map(on_device, mesh=fine, in_specs=placed, out_specs=P(IMG, FSDP), check_vma=False)
```

time: 565 us -> 180 us (0.32)
  waiting for transfers between devices: 444 us -> 58.4 us
  blocking collectives: 32 us -> 60.1 us
  other arithmetic: 27.5 us -> 4.62 us
  local copies, waits for them, and re-layouts: 18.3 us -> 3.37 us
  starting transfers between devices: 15.1 us -> 29.1 us
  matrix products: 12.9 us -> 0 us
  Pallas kernels: 0 us -> 9.19 us
    all_gather x3 -> x2, waiting for transfers between devices: 303 us -> 40.6 us  [the longest x1 40.6 us: on_device(): query_weights = lax.all_gather(w_query, 'j')]
    psum x1 -> x0, waiting for transfers between devices: 79.1 us -> none  [on_device(): query_raw = lax.psum(partial_query, 'img')]
    reduce_scatter x1 -> x0, waiting for transfers between devices: 40 us -> none  [on_device(): lax.psum_scatter(partial_out, 'img', scatter_dimension=0, tiled=True)]
    all_to_all x0 -> x1, blocking collectives: none -> 20.3 us  [on_device(): partial = lax.all_to_all(partial.reshape(8, 256, HD), IMG, 0, 0, tiled=True)]
    add x15 -> x0, other arithmetic: 15.5 us -> none  [the longest x7 15.4 us: pair_merge(): weighted_first * factor_first[..., None]]
    all_to_all x1 -> x3, starting transfers between devices: 14.9 us -> 29.1 us  [the longest x1 12.1 us: on_device(): lax.all_to_all(partial, NEAR + IMG, 0, 0, tiled=True).reshape(8, 8, 32, HD)]
    dot_general x4 -> x0, matrix products: 12.9 us -> none  [the longest x1 4.4 us: on_device(): jnp.dot(lax.all_gather(scaled, 'fsdp', axis=0, tiled=True), w_query, pref...]
    pallas_call x0 -> x4, Pallas kernels: none -> 9.19 us  [the longest x1 4.94 us: attend(): pl.pallas_call(kernel, in_specs=[SMEM, SMEM, SMEM, whole, whole], out_spe...]
  transfers between devices with their start and end apart: 6 -> 5, of which waited for: 6 -> 3; matrix products, arithmetic and copies ran while one was open for 2% -> 2% of each run, Pallas kernels for 0% -> 4%
where the time goes in v3:
time: 180 us; the launch traced here: 179 us
  blocking collectives  60.1 us (33%)
  waiting for transfers between devices  58.4 us (32%)
  starting transfers between devices  29.1 us (16%)
  between operations  14.2 us (8%)
  Pallas kernels  9.19 us (5%)
  other arithmetic  4.62 us (3%)
  local copies, waits for them, and re-layouts  3.37 us (2%)
    all_gather x1, waiting for transfers between devices, on_device(): query_weights = lax.all_gather(w_query, 'j')  40.6 us
    all_gather x1, blocking collectives, on_device(): attended = lax.all_gather(attended, 'j', axis=0, tiled=True)  24.9 us
    all_to_all x1, blocking collectives, on_device(): partial = lax.all_to_all(partial.reshape(8, 256, HD), IMG, 0, 0, tiled=True)  20.3 us
    all_gather x2, blocking collectives, on_device(): scaled = lax.all_gather(lax.all_gather(scaled, 's'), 'y')  14.9 us
    all_to_all x1, starting transfers between devices, on_device(): lax.all_to_all(partial, NEAR + IMG, 0, 0, tiled=True).reshape(8, 8, 32, HD)  12.1 us
    all_to_all x1, waiting for transfers between devices, on_device(): lax.all_to_all(partial, NEAR + IMG, 0, 0, tiled=True).reshape(8, 8, 32, HD)  11.5 us
    all_to_all x1, starting transfers between devices, on_device(): caches = lax.all_to_all(caches, IMG, 0, 0, tiled=True)  11.4 us
    all_to_all x1, waiting for transfers between devices, on_device(): lax.all_to_all(query.reshape(8, 32, HD), ('y', 's'), 0, 0, tiled=True)  5.62 us
  transfers between devices with their start and end apart: 5, of which 3 were waited for; matrix products, arithmetic and copies ran while one was open for 2% of the time, Pallas kernels for 4%

profile of v3, /device:TPU:1, one launch (start us, length us, event | category | flops | bytes accessed | tf_op | source)
XLA Modules:
  0.0 179.0 jit_solution(3746752733359617176)
XLA Ops:
  6.5 0.0 all-gather.7.cloned.1.call-start
  6.5 0.7 all-gather.7.cloned.1.call-update
  7.3 3.9 %bitcast_bitcast_fusion = bf16[8,2,1024,128]{3,2,1,0:T(8,128)(2,1)} fusion(bf16[1,1024,1024]{2,1,0:T(8,128)(2,1)} %param.16, bf16[1,1024,1024]{2,1,0:T(8,128)(2,1)} %param.15), kind=kLoop, calls=%fused_computation | loop fusion | flops 2097152 | bytes 8388608 | tf_op jit(solution)/shard_map/transpose | solution.py:153
  11.2 0.0 copy-start.4
  11.2 0.0 copy-start.5
  11.2 11.4 %all-to-all-start = ((bf16[8,2,1024,128]{3,2,1,0:T(8,128)(2,1)}), bf16[8,2,1024,128]{3,2,1,0:T(8,128)(2,1)}, u32[]{:S(2)}, u32[]{:S(2)}) async-start(bf16[8,2,1024,128]{3,2,1,0:T(8,128)(2,1)} %bitcast_bitcast_fusion), calls=%async_computation | async-start | bytes 8388608 | tf_op jit(solution)/shard_map/all_to_all | solution.py:155
  22.6 0.0 all-gather.9.cloned.1.call-start
  22.6 0.0 copy-done.4
  22.6 0.0 copy-done.5
  22.6 4.2 %all-gather = bf16[64,1024]{1,0:T(8,128)(2,1)S(1)} all-gather(bf16[32,1024]{1,0:T(8,128)(2,1)S(1)} %multiply_convert_fusion.1), channel_id=2, replica_groups=mesh['j'=8,'s'=2,'y'=4,'x'=4,'c'=2] {'s'}, dimensions={0}, use_global_device_ids=true | all-gather | bytes 196608 | tf_op jit(solution)/shard_map/all_gather | solution.py:157
  26.8 10.7 %all-gather.1 = bf16[8,32,1024]{2,1,0:T(8,128)(2,1)S(1)} all-gather(bf16[2,32,1024]{2,1,0:T(8,128)(2,1)S(1)} %bitcast.26), channel_id=3, replica_groups=mesh['j'=8,'s'=2,'y'=4,'x'=4,'c'=2] {'y'}, dimensions={0}, use_global_device_ids=true | all-gather | bytes 655360 | tf_op jit(solution)/shard_map/all_gather | solution.py:157
  37.5 40.6 %all-gather.7.cloned.1.call-done = bf16[8192,128]{1,0:T(8,128)(2,1)} async-done(((bf16[1024,128]{1,0:T(8,128)(2,1)}), bf16[8192,128]{1,0:T(8,128)(2,1)}) %all-gather.7.cloned.1.call-update) | async-done | bytes 2097168 | tf_op jit(solution)/shard_map/all_gather | solution.py:152
  78.1 0.0 copy-start
  78.1 1.6 copy-done
  79.7 1.3 shard_map.109
  80.9 0.0 copy-start.2
  81.0 0.0 copy-start.6
  81.0 0.0 copy-start.7
  81.0 0.0 copy-start.3
  81.0 0.0 all-to-all-done
  81.0 0.0 all-gather.9.cloned.1.call-update
  81.0 20.3 %all_to_all.20.part_ref = f32[8,256,128]{2,1,0:T(8,128)S(1)} all-to-all(f32[8,256,128]{2,1,0:T(8,128)S(1)} %shard_map.109), channel_id=1, replica_groups=mesh['j'=8,'s'=2,'y'=4,'x'=4,'c'=2] {'x','c'}, dimensions={0} | all-to-all | bytes 2097152 | tf_op jit(solution)/shard_map/all_to_all | solution.py:162
  101.3 0.0 copy-done.2
  101.3 0.8 shard_map.110
  102.1 5.6 %all-to-all-start.2 = ((bf16[8,32,128]{2,1,0:T(8,128)(2,1)}), bf16[8,32,128]{2,1,0:T(8,128)(2,1)S(1)}, u32[]{:S(2)}, u32[]{:S(2)}) async-start(bf16[8,32,128]{2,1,0:T(8,128)(2,1)} %bitcast.8), calls=%async_computation.2 | async-start | bytes 131072 | tf_op jit(solution)/shard_map/all_to_all | solution.py:164
  107.7 0.0 copy-done.6
  107.7 0.1 copy.17.marks_ref
  107.7 0.0 copy-done.7
  107.7 0.1 copy.16.slots_ref
  107.8 5.6 %all-to-all-done.2.query_ref = bf16[8,32,128]{2,1,0:T(8,128)(2,1)S(1)} async-done(((bf16[8,32,128]{2,1,0:T(8,128)(2,1)}), bf16[8,32,128]{2,1,0:T(8,128)(2,1)S(1)}, u32[]{:S(2)}, u32[]{:S(2)}) %all-to-all-start.2) | async-done | bytes 65568 | tf_op jit(solution)/shard_map/all_to_all | solution.py:164
  113.5 0.0 copy-done.3
  113.5 4.9 %shard_map.111 = bf16[32,1024]{1,0:T(8,128)(2,1)S(1)} custom-call(s32[8,2]{1,0:T(8,128)S(1)} %copy.16.slots_ref, s32[8]{0:T(128)S(1)} %copy-done.3, s32[32,8]{1,0:T(8,128)S(1)} %copy.17.marks_ref, bf16[8,32,128]{2,1,0:T(8,128)(2,1)S(1)} %all-to-all-done.2.query_ref, bf16[8,2,2,512,128]{4,3,2,1,0:T(8,128)(2,1)} %bitcast.9.cache_ref), custom_call_target="tpu_custom_call" | custom-call | flops 134217728 | bytes 5242880 | tf_op jit(solution)/shard_map/pallas_call | solution.py:129
  118.4 24.9 %all_gather.33.rows_ref = bf16[256,1024]{1,0:T(8,128)(2,1)S(1)} all-gather(bf16[32,1024]{1,0:T(8,128)(2,1)S(1)} %shard_map.111), channel_id=1, replica_groups=mesh['j'=8,'s'=2,'y'=4,'x'=4,'c'=2] {'j'}, dimensions={0}, use_global_device_ids=true | all-gather | bytes 589824 | tf_op jit(solution)/shard_map/all_gather | solution.py:167
  143.3 0.0 all-gather.9.cloned.1.call-done
  143.3 0.0 copy-start.1
  143.3 1.6 copy-done.1
  144.9 2.2 %shard_map.112 = bf16[8,256,128]{2,1,0:T(8,128)(2,1)} custom-call(bf16[256,1024]{1,0:T(8,128)(2,1)S(1)} %all_gather.33.rows_ref, bf16[8,1024,128]{2,1,0:T(8,128)(2,1)S(1)} %bitcast.24), custom_call_target="tpu_custom_call" | custom-call | flops 536870912 | bytes 4194304 | tf_op jit(solution)/shard_map/pallas_call | solution.py:46
  147.2 12.1 %all-to-all-start.3 = ((bf16[64,32,128]{2,1,0:T(8,128)(2,1)}), bf16[64,32,128]{2,1,0:T(8,128)(2,1)S(1)}, u32[]{:S(2)}, u32[]{:S(2)}) async-start(bf16[64,32,128]{2,1,0:T(8,128)(2,1)} %bitcast.11), calls=%async_computation.3 | async-start | bytes 1048576 | tf_op jit(solution)/shard_map/all_to_all | solution.py:169
  159.9 11.5 %all-to-all-done.3 = bf16[64,32,128]{2,1,0:T(8,128)(2,1)S(1)} async-done(((bf16[64,32,128]{2,1,0:T(8,128)(2,1)}), bf16[64,32,128]{2,1,0:T(8,128)(2,1)S(1)}, u32[]{:S(2)}, u32[]{:S(2)}) %all-to-all-start.3) | async-done | bytes 524320 | tf_op jit(solution)/shard_map/all_to_all | solution.py:169
  171.4 0.1 convert_reduce_fusion
  171.5 0.6 multiply_convert_fusion
  (1 shorter events, 0.0 us)
Async XLA Ops:
  6.5 71.6 %all-gather.7.cloned.1.call-start = ((), (), s32[]{:S(2)}) async-start(), calls=%async_computation.4 | async-start | bytes 2359296 | tf_op jit(solution)/shard_map/all_gather | solution.py:152
  11.2 11.4 %copy-start.4 = (bf16[32,1024]{1,0:T(8,128)(2,1)S(1)}, bf16[32,1024]{1,0:T(8,128)(2,1)}, u32[]{:S(2)}) copy-start(bf16[32,1024]{1,0:T(8,128)(2,1)} %param.11) | copy-start | bytes 196612
  11.2 11.4 %copy-start.5 = (f32[1024]{0:T(1024)S(1)}, f32[1024]{0:T(1024)}, u32[]{:S(2)}) copy-start(f32[1024]{0:T(1024)} %param.12) | copy-start | bytes 12292
  11.2 69.8 %all-to-all-start = ((bf16[8,2,1024,128]{3,2,1,0:T(8,128)(2,1)}), bf16[8,2,1024,128]{3,2,1,0:T(8,128)(2,1)}, u32[]{:S(2)}, u32[]{:S(2)}) async-start(bf16[8,2,1024,128]{3,2,1,0:T(8,128)(2,1)} %bitcast_bitcast_fusion), calls=%async_computation | async-start | bytes 8388608 | tf_op jit(solution)/shard_map/all_to_all | solution.py:155
  22.6 120.8 %all-gather.9.cloned.1.call-start = ((), (), s32[]{:S(2)}) async-start(), calls=%async_computation.5 | async-start | bytes 2359296 | tf_op jit(solution)/shard_map/all_gather | solution.py:161
  78.1 1.6 copy-start
  80.9 20.4 %copy-start.2 = (f32[128]{0:T(128)S(1)}, f32[128]{0:T(128)}, u32[]{:S(2)}) copy-start(f32[128]{0:T(128)} %param.14) | copy-start | bytes 1540
  81.0 26.7 %copy-start.6 = (s32[32,8]{0,1:T(8,128)S(1)}, s32[32,8]{0,1:T(8,128)}, u32[]{:S(2)}) copy-start(s32[32,8]{0,1:T(8,128)} %param.17) | copy-start | bytes 3076
  81.0 26.8 %copy-start.7 = (s32[8,2]{0,1:T(2,128)S(1)}, s32[8,2]{0,1:T(2,128)}, u32[]{:S(2)}) copy-start(s32[8,2]{0,1:T(2,128)} %param.19) | copy-start | bytes 196
  81.0 32.5 %copy-start.3 = (s32[8]{0:T(128)S(1)}, s32[8]{0:T(128)}, u32[]{:S(2)}) copy-start(s32[8]{0:T(128)} %counts_ref.1) | copy-start | bytes 100
  102.1 11.4 %all-to-all-start.2 = ((bf16[8,32,128]{2,1,0:T(8,128)(2,1)}), bf16[8,32,128]{2,1,0:T(8,128)(2,1)S(1)}, u32[]{:S(2)}, u32[]{:S(2)}) async-start(bf16[8,32,128]{2,1,0:T(8,128)(2,1)} %bitcast.8), calls=%async_computation.2 | async-start | bytes 131072 | tf_op jit(solution)/shard_map/all_to_all | solution.py:164
  143.3 1.6 copy-start.1
  147.2 24.3 %all-to-all-start.3 = ((bf16[64,32,128]{2,1,0:T(8,128)(2,1)}), bf16[64,32,128]{2,1,0:T(8,128)(2,1)S(1)}, u32[]{:S(2)}, u32[]{:S(2)}) async-start(bf16[64,32,128]{2,1,0:T(8,128)(2,1)} %bitcast.11), calls=%async_computation.3 | async-start | bytes 1048576 | tf_op jit(solution)/shard_map/all_to_all | solution.py:169
Sparse Core Ops, SparseCore 0:
  9.4 68.6 all-gather.6
  81.1 40.7 all-gather.8

commit v4 on v3

v4 whole, which is shorter than its diff:
```python
import functools

import jax
import jax.numpy as jnp
from jax import lax
from jax.experimental import pallas as pl
from jax.experimental.pallas import tpu as pltpu
from jax.sharding import Mesh
from jax.sharding import PartitionSpec as P

H = 64
KVH = 8
HD = 128
IMG_BLK = 4
BLOCK_TOK = 128
IMG_TOK = 512
STEPS = 4

NEGATIVE = -1e30
EPSILON = 1e-05

BF16 = jnp.bfloat16
F32 = jnp.float32
MIB = 1 << 20

AXES = ("j", "s", "y", "x", "c")
SIZES = (8, 2, 4, 4, 2)
NEAR = ("s", "y")
IMG = ("x", "c")
FSDP = ("j", "s", "y")

SMEM = pl.BlockSpec(memory_space=pltpu.SMEM)


def cost(flops, size, exps=0):
    return pl.CostEstimate(flops=flops, bytes_accessed=size, transcendentals=exps)


def query_product(core, rows, weights):
    def kernel(core_ref, rows_ref, weight_ref, own_ref, other_ref):
        value = rows_ref[...].reshape(256, 1024)
        for pair in range(4):
            weight = jnp.concatenate([weight_ref[2 * pair], weight_ref[2 * pair + 1]], axis=1)
            total = jnp.dot(value, weight, preferred_element_type=F32).reshape(8, 32, 2 * HD)
            first, second = total[:, :, :HD], total[:, :, HD:]
            own_ref[:, pair] = jnp.where(core_ref[0] == 0, first, second)
            other_ref[:, pair] = jnp.where(core_ref[0] == 0, second, first)

    shape = jax.ShapeDtypeStruct((8, 4, 32, HD), F32)
    whole = pl.BlockSpec(memory_space=pltpu.VMEM)
    return pl.pallas_call(
        kernel,
        in_specs=[SMEM, whole, whole],
        out_specs=[whole, whole],
        out_shape=(shape, shape),
        compiler_params=pltpu.CompilerParams(vmem_limit_bytes=24 * MIB),
        cost_estimate=cost(2 * 256 * 1024 * 1024, 4 * MIB),
    )(core, rows, weights)


def out_product(core, spot, rows, weights):
    def kernel(core_ref, spot_ref, rows_ref, *refs):
        *weight_refs, own_ref, other_ref = refs
        value = rows_ref[...].reshape(256, 1024)
        for back, weight_ref in enumerate(weight_refs):
            weight = jnp.concatenate([weight_ref[0], weight_ref[1]], axis=1)
            total = jnp.dot(value, weight, preferred_element_type=F32).reshape(4, 2, 32, 2 * HD)
            own = jnp.where(core_ref[0] == 0, total[:, 0], total[:, 1])
            other = jnp.where(core_ref[0] == 0, total[:, 1], total[:, 0])
            place = lax.rem(spot_ref[0] + 4 - back, 4)
            for s in range(2):
                own_ref[place, s] = own[:, :, s * HD : (s + 1) * HD]
                other_ref[place, s] = other[:, :, s * HD : (s + 1) * HD]

    shape = jax.ShapeDtypeStruct((4, 2, 4, 32, HD), F32)
    whole = pl.BlockSpec(memory_space=pltpu.VMEM)
    return pl.pallas_call(
        kernel,
        in_specs=[SMEM, SMEM] + [whole] * 5,
        out_specs=[whole, whole],
        out_shape=(shape, shape),
        compiler_params=pltpu.CompilerParams(vmem_limit_bytes=24 * MIB),
        cost_estimate=cost(2 * 256 * 1024 * 1024, 4 * MIB),
    )(core, spot, rows, *weights)


def attend(slots, marks, parts, gain, caches):
    def kernel(slots_ref, marks_ref, part_ref, gain_ref, cache_ref, out_ref, score_ref, expo_ref):
        low = lax.broadcasted_iota(jnp.int32, (8, HD), 0) < 4
        places = []
        for s in range(8):
            slot = [jnp.clip(slots_ref[s, k], 0, 15) for k in range(2)]
            places.append([(one // 2, one % 2) for one in slot])
        heads = []
        for h in range(8):
            value = jnp.sum(part_ref[h % 4 * 2 + h // 4], axis=0)
            inverse = lax.rsqrt(jnp.mean(value * value, axis=-1, keepdims=True) + EPSILON)
            heads.append(value * inverse * gain_ref[...])
        for s in range(8):
            tiles = []
            for h in range(0, 8, 2):
                even, odd = (head[s // 2 * 8 : s // 2 * 8 + 8] for head in heads[h : h + 2])
                if s % 2 == 0:
                    tiles.append(jnp.where(low, even, pltpu.roll(odd, 4, 0)))
                else:
                    tiles.append(jnp.where(low, pltpu.roll(even, 4, 0), odd))
            rows = jnp.concatenate(tiles, axis=0).astype(BF16)
            for k in range(2):
                score_ref[s, :, k * IMG_TOK : (k + 1) * IMG_TOK] = lax.dot_general(
                    rows,
                    cache_ref[places[s][k][0], 0, places[s][k][1]],
                    (((1,), (1,)), ((), ())),
                    preferred_element_type=F32,
                )
        totals = []
        for s in range(8):
            blocks = [
                jnp.broadcast_to(marks_ref[8 * s : 8 * s + 8, b : b + 1], (8, BLOCK_TOK)) for b in range(2 * IMG_BLK)
            ]
            visible = (jnp.concatenate(blocks, axis=1) > 0.5).reshape(1, 8, 2 * IMG_TOK)
            score = (score_ref[s] * HD ** (-0.5)).reshape(4, 8, 2 * IMG_TOK)
            peak = jnp.max(jnp.where(visible, score, NEGATIVE), axis=-1, keepdims=True)
            expo = jnp.where(visible, jnp.exp(score - peak), 0.0)
            totals.append(jnp.sum(expo, axis=-1, keepdims=True))
            expo_ref[s] = expo.reshape(32, 2 * IMG_TOK).astype(BF16)
        results = []
        for s in range(8):
            first, second = (cache_ref[place[0], 1, place[1]] for place in places[s])
            weighted = jnp.dot(expo_ref[s, :, :IMG_TOK], first, preferred_element_type=F32)
            weighted += jnp.dot(expo_ref[s, :, IMG_TOK:], second, preferred_element_type=F32)
            results.append(weighted.reshape(4, 8, HD) / totals[s])
        for h in range(8):
            tiles = []
            for pair in range(4):
                even, odd = results[2 * pair][h // 2], results[2 * pair + 1][h // 2]
                if h % 2 == 0:
                    tiles.append(jnp.where(low, even, pltpu.roll(odd, 4, 0)))
                else:
                    tiles.append(jnp.where(low, pltpu.roll(even, 4, 0), odd))
            tile = jnp.concatenate(tiles, axis=0).astype(BF16)
            out_ref[:, h * HD : (h + 1) * HD] = tile

    whole = pl.BlockSpec(memory_space=pltpu.VMEM)
    return pl.pallas_call(
        kernel,
        in_specs=[SMEM, whole, whole, whole, whole],
        out_specs=whole,
        out_shape=jax.ShapeDtypeStruct((32, KVH * HD), BF16),
        scratch_shapes=[pltpu.VMEM((8, 32, 2 * IMG_TOK), F32), pltpu.VMEM((8, 32, 2 * IMG_TOK), BF16)],
        compiler_params=pltpu.CompilerParams(vmem_limit_bytes=24 * MIB),
        cost_estimate=cost(4 * 2 * 32 * 8 * 512 * 128, 5 * MIB, 2 * 8 * 32 * 512),
    )(slots, marks, parts, gain, caches)


def on_device(
    tokens,
    norm_gain,
    w_query,
    query_gain,
    key_cache,
    value_cache,
    block_mask,
    image_counts,
    image_slot,
    attn_gate,
    w_out,
):
    query_weights = lax.all_gather(w_query, "j")
    caches = jnp.stack([key_cache[0], value_cache[0]]).reshape(2, 1024, KVH, HD).transpose(2, 0, 1, 3)
    caches, tokens = lax.optimization_barrier((caches, tokens))
    caches = lax.all_to_all(caches, IMG, 0, 0, tiled=True)
    scaled = (tokens.astype(F32) * norm_gain).astype(BF16)
    scaled = lax.all_gather(lax.all_gather(scaled, "s"), "y")
    out_weights = [lax.all_gather(w_out, "s")]
    for ahead in range(1, 4):
        out_weights.append(lax.ppermute(out_weights[0], "y", [(a, (a + ahead) % 4) for a in range(4)]))
    live = jnp.arange(2, dtype=jnp.int32)[None, :] < image_counts[:, None]
    marks = (block_mask.reshape(8, STEPS, 2, IMG_BLK) == 1) & live[:, None, :, None]
    marks = jnp.tile(marks.reshape(8, STEPS, 2 * IMG_BLK).astype(F32), (1, 2, 1)).reshape(64, 2 * IMG_BLK)
    scaled, out_weights, marks = lax.optimization_barrier((scaled, out_weights, marks))

    core = lax.axis_index("c").reshape(1)
    swap = [(0, 1), (1, 0)]
    own, other = query_product(core, scaled.reshape(8, 32, 1024), query_weights)
    own, caches = lax.optimization_barrier((own, caches))
    parts = (own + lax.ppermute(other, "c", swap)).reshape(32, 32, HD)
    parts = lax.all_to_all(parts, ("y", "s", "x"), 0, 0, tiled=True).reshape(8, 4, 32, HD)
    caches = caches.reshape(8, 2, 2, IMG_TOK, HD)
    attended = attend(image_slot, marks, parts, query_gain.reshape(1, HD), caches)

    spot = lax.axis_index("y").reshape(1)
    own, other = out_product(core, spot, lax.all_gather(attended, "j"), out_weights)
    partial = (own + lax.ppermute(other, "c", swap)).astype(BF16).reshape(32, 32, HD)
    partial = lax.all_to_all(partial, ("y", "s", "x"), 0, 0, tiled=True).reshape(4, 2, 4, 32, HD)
    mixed = (jnp.tanh(attn_gate[0]) * jnp.sum(partial.astype(F32), axis=2)).astype(BF16)
    return mixed.swapaxes(0, 1).reshape(256, HD)


def solution(mesh):
    fine = Mesh(mesh.devices.reshape(SIZES), AXES)
    placed = (
        P(FSDP, IMG),
        P(IMG),
        P(IMG, FSDP),
        P(),
        P(FSDP, IMG, None),
        P(FSDP, IMG, None),
        P(FSDP, None),
        P(FSDP),
        P(FSDP, None),
        P(),
        P(IMG, FSDP),
    )
    return jax.shard_map(on_device, mesh=fine, in_specs=placed, out_specs=P(IMG, FSDP), check_vma=False)
```

time: 180 us -> 169 us (0.939)
  waiting for transfers between devices: 58.4 us -> 31.8 us
  starting transfers between devices: 29.1 us -> 44.5 us
  Pallas kernels: 9.19 us -> 5.87 us
  blocking collectives: 60.1 us -> 63.3 us
    all_gather x1, waiting for transfers between devices: 40.6 us -> 10.4 us  [on_device(): query_weights = lax.all_gather(w_query, 'j')]
    ppermute x0 -> x5, starting transfers between devices: none -> 22.7 us  [the longest x1 9.74 us: on_device(): lax.ppermute(other, 'c', swap)]
    all_to_all x1 -> x0, blocking collectives: 20.3 us -> none  [on_device(): partial = lax.all_to_all(partial.reshape(8, 256, HD), IMG, 0, 0, tiled=True)]
    all_gather x2, blocking collectives: 14.9 us -> 28.8 us  [on_device(): scaled = lax.all_gather(lax.all_gather(scaled, 's'), 'y')]
    all_gather x1 -> x2, blocking collectives: 24.9 us -> 34.5 us  [the longest x1 25.7 us: on_device(): lax.all_gather(attended, 'j')]
    all_to_all x2, starting transfers between devices: 17.7 us -> 10.4 us  [the longest x1 6.54 us: on_device(): lax.all_to_all(parts, ('y', 's', 'x'), 0, 0, tiled=True)]
    pallas_call x4 -> x3, Pallas kernels: 9.19 us -> 5.87 us  [the longest x1 3.59 us: attend(): pl.pallas_call(kernel, in_specs=[SMEM, whole, whole, whole, whole], out_s...]
    ppermute x0 -> x5, waiting for transfers between devices: none -> 3.24 us  [the longest x1 1.71 us: on_device(): parts = (own + lax.ppermute(other, 'c', swap)).reshape(32, 32, HD)]
  transfers between devices with their start and end apart: 5 -> 9, of which waited for: 3 -> 5; matrix products, arithmetic and copies ran while one was open for 2% -> 3% of each run, Pallas kernels for 4% -> 1%
where the time goes in v4:
time: 169 us; the launch traced here: 168 us
  blocking collectives  63.3 us (37%)
  starting transfers between devices  44.5 us (26%)
  waiting for transfers between devices  31.8 us (19%)
  between operations  14.3 us (8%)
  Pallas kernels  5.87 us (3%)
  other arithmetic  5.67 us (3%)
  local copies, waits for them, and re-layouts  2.51 us (1%)
    all_gather x2, blocking collectives, on_device(): scaled = lax.all_gather(lax.all_gather(scaled, 's'), 'y')  28.8 us
    all_gather x1, blocking collectives, on_device(): lax.all_gather(attended, 'j')  25.7 us
    all_to_all x1, starting transfers between devices, on_device(): caches = lax.all_to_all(caches, IMG, 0, 0, tiled=True)  11.5 us
    all_gather x1, waiting for transfers between devices, on_device(): query_weights = lax.all_gather(w_query, 'j')  10.4 us
    all_to_all x1, waiting for transfers between devices, on_device(): lax.all_to_all(parts, ('y', 's', 'x'), 0, 0, tiled=True)  10.1 us
    ppermute x1, starting transfers between devices, on_device(): lax.ppermute(other, 'c', swap)  9.74 us
    all_gather x1, blocking collectives, on_device(): out_weights = [lax.all_gather(w_out, 's')]  8.83 us
    ppermute x3, starting transfers between devices, on_device(): lax.ppermute(out_weights[0], 'y', [(a, (a + ahead) % 4) for a in range(4)])  8.4 us
  transfers between devices with their start and end apart: 9, of which 5 were waited for; matrix products, arithmetic and copies ran while one was open for 3% of the time, Pallas kernels for 1%

profile of v4, /device:TPU:1, one launch (start us, length us, event | category | flops | bytes accessed | tf_op | source)
XLA Modules:
  0.0 168.0 jit_solution(16169246896036838389)
XLA Ops:
  6.5 0.0 all-gather.7.cloned.1.call-start
  6.5 0.7 all-gather.7.cloned.1.call-update
  7.3 3.9 %bitcast_bitcast_fusion = bf16[8,2,1024,128]{3,2,1,0:T(8,128)(2,1)} fusion(bf16[1,1024,1024]{2,1,0:T(8,128)(2,1)} %param.16, bf16[1,1024,1024]{2,1,0:T(8,128)(2,1)} %param.15), kind=kLoop, calls=%fused_computation | loop fusion | flops 2097152 | bytes 8388608 | tf_op jit(solution)/shard_map/transpose | solution.py:169
  11.2 0.0 copy-start.2
  11.2 0.0 copy-start.3
  11.2 0.0 copy-start.4
  11.2 0.0 copy-start.7
  11.2 0.0 copy-start.5
  11.2 11.5 %all-to-all-start = ((bf16[8,2,1024,128]{3,2,1,0:T(8,128)(2,1)}), bf16[8,2,1024,128]{3,2,1,0:T(8,128)(2,1)}, u32[]{:S(2)}, u32[]{:S(2)}) async-start(bf16[8,2,1024,128]{3,2,1,0:T(8,128)(2,1)} %bitcast_bitcast_fusion), calls=%async_computation | async-start | bytes 8388608 | tf_op jit(solution)/shard_map/all_to_all | solution.py:171
  22.7 0.0 copy-done.2
  22.7 0.0 copy-start.6
  22.7 0.0 copy-start.1
  22.7 8.8 %all-gather.2 = bf16[2048,128]{1,0:T(8,128)(2,1)S(1)} all-gather(bf16[1024,128]{1,0:T(8,128)(2,1)S(1)} %copy-done.2), channel_id=4, replica_groups=mesh['j'=8,'s'=2,'y'=4,'x'=4,'c'=2] {'s'}, dimensions={0}, use_global_device_ids=true | all-gather | bytes 786432 | tf_op jit(solution)/shard_map/all_gather | solution.py:174
  31.5 1.9 %collective-permute-start = (bf16[2,1024,128]{2,1,0:T(8,128)(2,1)S(1)}, bf16[2,1024,128]{2,1,0:T(8,128)(2,1)S(1)}, u32[]{:S(2)}, u32[]{:S(2)}) collective-permute-start(bf16[2,1024,128]{2,1,0:T(8,128)(2,1)S(1)} %bitcast.30), channel_id=1, source_target_pairs={{0,8},{8,16},{16,24},{24,0},{1,9},{9,17},{17,25},{25,1},{2,10},{10... | collective-permute-start | bytes 1572872 | tf_op jit(solution)/shard_map/ppermute | solution.py:176
  33.4 1.9 %collective-permute-start.1 = (bf16[2,1024,128]{2,1,0:T(8,128)(2,1)S(1)}, bf16[2,1024,128]{2,1,0:T(8,128)(2,1)S(1)}, u32[]{:S(2)}, u32[]{:S(2)}) collective-permute-start(bf16[2,1024,128]{2,1,0:T(8,128)(2,1)S(1)} %bitcast.31), channel_id=1, source_target_pairs={{0,16},{8,24},{16,0},{24,8},{1,17},{9,25},{17,1},{25,9},{2,18},{10... | collective-permute-start | bytes 1572872 | tf_op jit(solution)/shard_map/ppermute | solution.py:176
  35.3 4.6 %collective-permute-start.2 = (bf16[2,1024,128]{2,1,0:T(8,128)(2,1)S(1)}, bf16[2,1024,128]{2,1,0:T(8,128)(2,1)S(1)}, u32[]{:S(2)}, u32[]{:S(2)}) collective-permute-start(bf16[2,1024,128]{2,1,0:T(8,128)(2,1)S(1)} %bitcast.32), channel_id=1, source_target_pairs={{0,24},{8,0},{16,8},{24,16},{1,25},{9,1},{17,9},{25,17},{2,26},{10... | collective-permute-start | bytes 1572872 | tf_op jit(solution)/shard_map/ppermute | solution.py:176
  39.9 0.0 copy-done.3
  39.9 0.0 copy-done.4
  40.0 6.0 %all-gather = bf16[64,1024]{1,0:T(8,128)(2,1)S(1)} all-gather(bf16[32,1024]{1,0:T(8,128)(2,1)S(1)} %multiply_convert_fusion.1), channel_id=2, replica_groups=mesh['j'=8,'s'=2,'y'=4,'x'=4,'c'=2] {'s'}, dimensions={0}, use_global_device_ids=true | all-gather | bytes 196608 | tf_op jit(solution)/shard_map/all_gather | solution.py:173
  46.0 0.0 copy-done.7
  46.0 22.8 %all-gather.1 = bf16[8,32,1024]{2,1,0:T(8,128)(2,1)S(1)} all-gather(bf16[2,32,1024]{2,1,0:T(8,128)(2,1)S(1)} %bitcast.40), channel_id=3, replica_groups=mesh['j'=8,'s'=2,'y'=4,'x'=4,'c'=2] {'y'}, dimensions={0}, use_global_device_ids=true | all-gather | bytes 655360 | tf_op jit(solution)/shard_map/all_gather | solution.py:173
  68.8 0.0 copy-done.5
  68.8 0.1 copy.24
  68.9 0.1 copy.25
  69.0 0.0 collective-permute-done.refs_1_
  69.0 0.0 collective-permute-done.1.refs_2_
  69.0 0.0 collective-permute-done.2.refs_3_
  69.0 10.4 %all-gather.7.cloned.1.call-done = bf16[8192,128]{1,0:T(8,128)(2,1)} async-done(((bf16[1024,128]{1,0:T(8,128)(2,1)}), bf16[8192,128]{1,0:T(8,128)(2,1)}) %all-gather.7.cloned.1.call-update) | async-done | bytes 2097168 | tf_op jit(solution)/shard_map/all_gather | solution.py:168
  79.5 1.6 copy-done
  81.1 1.6 shard_map.109
  82.6 4.5 %collective-permute-start.3 = (f32[8,4,32,128]{3,2,1,0:T(8,128)}, f32[8,4,32,128]{3,2,1,0:T(8,128)S(1)}, u32[]{:S(2)}, u32[]{:S(2)}) collective-permute-start(f32[8,4,32,128]{3,2,1,0:T(8,128)} %get-tuple-element.25), channel_id=1, source_target_pairs={{0,1},{1,0},{2,3},{3,2},{4,5},{5,4},{6,7},{7,6},{8,9},{9,8},{10,11... | collective-permute-start | bytes 1572872 | tf_op jit(solution)/shard_map/ppermute | solution.py:186
  87.1 0.0 all-to-all-done
  87.2 1.7 %collective-permute-done.3 = f32[8,4,32,128]{3,2,1,0:T(8,128)S(1)} collective-permute-done((f32[8,4,32,128]{3,2,1,0:T(8,128)}, f32[8,4,32,128]{3,2,1,0:T(8,128)S(1)}, u32[]{:S(2)}, u32[]{:S(2)}) %collective-permute-start.3) | collective-permute-done | bytes 524320 | tf_op jit(solution)/shard_map/ppermute | solution.py:186
  88.9 0.9 add.6
  89.8 6.5 %all-to-all-start.1 = ((f32[32,32,128]{2,1,0:T(8,128)}), f32[32,32,128]{2,1,0:T(8,128)S(1)}, u32[]{:S(2)}, u32[]{:S(2)}) async-start(f32[32,32,128]{2,1,0:T(8,128)} %bitcast.39), calls=%async_computation.1 | async-start | bytes 1048576 | tf_op jit(solution)/shard_map/all_to_all | solution.py:187
  96.3 0.0 copy-done.6
  96.3 0.1 copy.26.slots_ref
  96.4 10.1 %all-to-all-done.1 = f32[32,32,128]{2,1,0:T(8,128)S(1)} async-done(((f32[32,32,128]{2,1,0:T(8,128)}), f32[32,32,128]{2,1,0:T(8,128)S(1)}, u32[]{:S(2)}, u32[]{:S(2)}) %all-to-all-start.1) | async-done | bytes 524320 | tf_op jit(solution)/shard_map/all_to_all | solution.py:187
  106.5 0.0 copy-done.1
  106.5 3.6 %shard_map.110 = bf16[32,1024]{1,0:T(8,128)(2,1)S(1)} custom-call(s32[8,2]{1,0:T(8,128)S(1)} %copy.26.slots_ref, f32[64,8]{1,0:T(8,128)S(1)} %bitcast.37, f32[8,4,32,128]{3,2,1,0:T(8,128)S(1)} %bitcast.34, f32[1,128]{1,0:T(1,128)S(1)} %bitcast.38, bf16[8,2,2,512,128]{4,3,2,1,0:T(8,128)(2,1)} %bitcast.15.cache_ref), custom_call_target="tpu_custom_call" | custom-call | flops 134217728 | bytes 5242880 | tf_op jit(solution)/shard_map/pallas_call | solution.py:144
  110.1 25.7 %all-gather.4 = bf16[256,1024]{1,0:T(8,128)(2,1)S(1)} all-gather(bf16[32,1024]{1,0:T(8,128)(2,1)S(1)} %shard_map.110), channel_id=6, replica_groups=mesh['j'=8,'s'=2,'y'=4,'x'=4,'c'=2] {'j'}, dimensions={0}, use_global_device_ids=true | all-gather | bytes 589824 | tf_op jit(solution)/shard_map/all_gather | solution.py:192
  135.8 0.7 shard_map.111
  136.5 9.7 %collective-permute-start.4 = (f32[4,2,4,32,128]{4,3,2,1,0:T(8,128)S(1)}, f32[4,2,4,32,128]{4,3,2,1,0:T(8,128)S(1)}, u32[]{:S(2)}, u32[]{:S(2)}) collective-permute-start(f32[4,2,4,32,128]{4,3,2,1,0:T(8,128)S(1)} %get-tuple-element.32), channel_id=1, source_target_pairs={{0,1},{1,0},{2,3},{3,2},{4,5},{5,4},{6,7},{7,6},{8,9},{9,8},{10,11... | collective-permute-start | bytes 1572872 | tf_op jit(solution)/shard_map/ppermute | solution.py:193
  146.3 1.5 collective-permute-done.4
  147.8 0.8 add_convert_fusion
  148.6 3.9 %all-to-all-start.2 = ((bf16[32,32,128]{2,1,0:T(8,128)(2,1)}), bf16[32,32,128]{2,1,0:T(8,128)(2,1)S(1)}, u32[]{:S(2)}, u32[]{:S(2)}) async-start(bf16[32,32,128]{2,1,0:T(8,128)(2,1)} %bitcast.17), calls=%async_computation.2 | async-start | bytes 524288 | tf_op jit(solution)/shard_map/all_to_all | solution.py:194
  153.1 7.4 %all-to-all-done.2 = bf16[32,32,128]{2,1,0:T(8,128)(2,1)S(1)} async-done(((bf16[32,32,128]{2,1,0:T(8,128)(2,1)}), bf16[32,32,128]{2,1,0:T(8,128)(2,1)S(1)}, u32[]{:S(2)}, u32[]{:S(2)}) %all-to-all-start.2) | async-done | bytes 262176 | tf_op jit(solution)/shard_map/all_to_all | solution.py:194
  160.5 0.6 copy.27
  (9 shorter events, 0.1 us)
Async XLA Ops:
  6.5 72.9 %all-gather.7.cloned.1.call-start = ((), (), s32[]{:S(2)}) async-start(), calls=%async_computation.3 | async-start | bytes 2359296 | tf_op jit(solution)/shard_map/all_gather | solution.py:168
  11.2 11.5 %copy-start.2 = (bf16[1024,128]{1,0:T(8,128)(2,1)S(1)}, bf16[1024,128]{1,0:T(8,128)(2,1)}, u32[]{:S(2)}) copy-start(bf16[1024,128]{1,0:T(8,128)(2,1)} %param.21) | copy-start | bytes 786436
  11.2 28.8 %copy-start.3 = (bf16[32,1024]{1,0:T(8,128)(2,1)S(1)}, bf16[32,1024]{1,0:T(8,128)(2,1)}, u32[]{:S(2)}) copy-start(bf16[32,1024]{1,0:T(8,128)(2,1)} %param.11) | copy-start | bytes 196612
  11.2 28.8 %copy-start.4 = (f32[1024]{0:T(1024)S(1)}, f32[1024]{0:T(1024)}, u32[]{:S(2)}) copy-start(f32[1024]{0:T(1024)} %param.12) | copy-start | bytes 12292
  11.2 34.8 %copy-start.7 = (s32[8]{0:T(128)S(1)}, s32[8]{0:T(128)}, u32[]{:S(2)}) copy-start(s32[8]{0:T(128)} %param.18) | copy-start | bytes 100
  11.2 57.6 %copy-start.5 = (s32[32,8]{0,1:T(8,128)S(1)}, s32[32,8]{0,1:T(8,128)}, u32[]{:S(2)}) copy-start(s32[32,8]{0,1:T(8,128)} %param.17) | copy-start | bytes 3076
  11.2 75.9 %all-to-all-start = ((bf16[8,2,1024,128]{3,2,1,0:T(8,128)(2,1)}), bf16[8,2,1024,128]{3,2,1,0:T(8,128)(2,1)}, u32[]{:S(2)}, u32[]{:S(2)}) async-start(bf16[8,2,1024,128]{3,2,1,0:T(8,128)(2,1)} %bitcast_bitcast_fusion), calls=%async_computation | async-start | bytes 8388608 | tf_op jit(solution)/shard_map/all_to_all | solution.py:171
  22.7 73.7 %copy-start.6 = (s32[8,2]{0,1:T(2,128)S(1)}, s32[8,2]{0,1:T(2,128)}, u32[]{:S(2)}) copy-start(s32[8,2]{0,1:T(2,128)} %param.19) | copy-start | bytes 196
  22.7 83.8 %copy-start.1 = (f32[128]{0:T(128)S(1)}, f32[128]{0:T(128)}, u32[]{:S(2)}) copy-start(f32[128]{0:T(128)} %param.14) | copy-start | bytes 1540
  31.5 37.5 %collective-permute-start = (bf16[2,1024,128]{2,1,0:T(8,128)(2,1)S(1)}, bf16[2,1024,128]{2,1,0:T(8,128)(2,1)S(1)}, u32[]{:S(2)}, u32[]{:S(2)}) collective-permute-start(bf16[2,1024,128]{2,1,0:T(8,128)(2,1)S(1)} %bitcast.30), channel_id=1, source_target_pairs={{0,8},{8,16},{16,24},{24,0},{1,9},{9,17},{17,25},{25,1},{2,10},{10... | collective-permute-start | bytes 1572872 | tf_op jit(solution)/shard_map/ppermute | solution.py:176
  33.4 35.6 %collective-permute-start.1 = (bf16[2,1024,128]{2,1,0:T(8,128)(2,1)S(1)}, bf16[2,1024,128]{2,1,0:T(8,128)(2,1)S(1)}, u32[]{:S(2)}, u32[]{:S(2)}) collective-permute-start(bf16[2,1024,128]{2,1,0:T(8,128)(2,1)S(1)} %bitcast.31), channel_id=1, source_target_pairs={{0,16},{8,24},{16,0},{24,8},{1,17},{9,25},{17,1},{25,9},{2,18},{10... | collective-permute-start | bytes 1572872 | tf_op jit(solution)/shard_map/ppermute | solution.py:176
  35.3 33.7 %collective-permute-start.2 = (bf16[2,1024,128]{2,1,0:T(8,128)(2,1)S(1)}, bf16[2,1024,128]{2,1,0:T(8,128)(2,1)S(1)}, u32[]{:S(2)}, u32[]{:S(2)}) collective-permute-start(bf16[2,1024,128]{2,1,0:T(8,128)(2,1)S(1)} %bitcast.32), channel_id=1, source_target_pairs={{0,24},{8,0},{16,8},{24,16},{1,25},{9,1},{17,9},{25,17},{2,26},{10... | collective-permute-start | bytes 1572872 | tf_op jit(solution)/shard_map/ppermute | solution.py:176
  79.5 1.6 copy-start
  82.6 6.2 %collective-permute-start.3 = (f32[8,4,32,128]{3,2,1,0:T(8,128)}, f32[8,4,32,128]{3,2,1,0:T(8,128)S(1)}, u32[]{:S(2)}, u32[]{:S(2)}) collective-permute-start(f32[8,4,32,128]{3,2,1,0:T(8,128)} %get-tuple-element.25), channel_id=1, source_target_pairs={{0,1},{1,0},{2,3},{3,2},{4,5},{5,4},{6,7},{7,6},{8,9},{9,8},{10,11... | collective-permute-start | bytes 1572872 | tf_op jit(solution)/shard_map/ppermute | solution.py:186
  89.8 16.7 %all-to-all-start.1 = ((f32[32,32,128]{2,1,0:T(8,128)}), f32[32,32,128]{2,1,0:T(8,128)S(1)}, u32[]{:S(2)}, u32[]{:S(2)}) async-start(f32[32,32,128]{2,1,0:T(8,128)} %bitcast.39), calls=%async_computation.1 | async-start | bytes 1048576 | tf_op jit(solution)/shard_map/all_to_all | solution.py:187
  136.5 11.3 %collective-permute-start.4 = (f32[4,2,4,32,128]{4,3,2,1,0:T(8,128)S(1)}, f32[4,2,4,32,128]{4,3,2,1,0:T(8,128)S(1)}, u32[]{:S(2)}, u32[]{:S(2)}) collective-permute-start(f32[4,2,4,32,128]{4,3,2,1,0:T(8,128)S(1)} %get-tuple-element.32), channel_id=1, source_target_pairs={{0,1},{1,0},{2,3},{3,2},{4,5},{5,4},{6,7},{7,6},{8,9},{9,8},{10,11... | collective-permute-start | bytes 1572872 | tf_op jit(solution)/shard_map/ppermute | solution.py:193
  148.6 11.9 %all-to-all-start.2 = ((bf16[32,32,128]{2,1,0:T(8,128)(2,1)}), bf16[32,32,128]{2,1,0:T(8,128)(2,1)S(1)}, u32[]{:S(2)}, u32[]{:S(2)}) async-start(bf16[32,32,128]{2,1,0:T(8,128)(2,1)} %bitcast.17), calls=%async_computation.2 | async-start | bytes 524288 | tf_op jit(solution)/shard_map/all_to_all | solution.py:194
Sparse Core Ops, SparseCore 0:
  9.4 69.9 all-gather.6

commit v5 on v4

--- a/solution.py
+++ b/solution.py
@@ -36,26 +36,29 @@
     return pl.CostEstimate(flops=flops, bytes_accessed=size, transcendentals=exps)
 
 
-def query_product(core, rows, weights):
-    def kernel(core_ref, rows_ref, weight_ref, own_ref, other_ref):
+def query_product(core, rows, weights, *sent):
+    def kernel(core_ref, rows_ref, weight_ref, *refs):
+        *sent_refs, out_ref = refs
         value = rows_ref[...].reshape(256, 1024)
-        for pair in range(4):
-            weight = jnp.concatenate([weight_ref[2 * pair], weight_ref[2 * pair + 1]], axis=1)
+        for pair in (0, 2):
+            first, second = weight_ref[2 * pair + core_ref[0]], weight_ref[2 * pair + 2 + core_ref[0]]
+            weight = jnp.concatenate([first, second], axis=1)
             total = jnp.dot(value, weight, preferred_element_type=F32).reshape(8, 32, 2 * HD)
-            first, second = total[:, :, :HD], total[:, :, HD:]
-            own_ref[:, pair] = jnp.where(core_ref[0] == 0, first, second)
-            other_ref[:, pair] = jnp.where(core_ref[0] == 0, second, first)
-
-    shape = jax.ShapeDtypeStruct((8, 4, 32, HD), F32)
+            for n in range(2):
+                part = total[:, :, n * HD : (n + 1) * HD]
+                for sent_ref in sent_refs:
+                    part = part + sent_ref[:, pair + n]
+                out_ref[:, pair + n] = part
+
     whole = pl.BlockSpec(memory_space=pltpu.VMEM)
     return pl.pallas_call(
         kernel,
-        in_specs=[SMEM, whole, whole],
-        out_specs=[whole, whole],
-        out_shape=(shape, shape),
+        in_specs=[SMEM, whole, whole] + [whole] * len(sent),
+        out_specs=whole,
+        out_shape=jax.ShapeDtypeStruct((8, 4, 32, HD), F32),
         compiler_params=pltpu.CompilerParams(vmem_limit_bytes=24 * MIB),
-        cost_estimate=cost(2 * 256 * 1024 * 1024, 4 * MIB),
-    )(core, rows, weights)
+        cost_estimate=cost(256 * 1024 * 1024, 2 * MIB),
+    )(core, rows, weights, *sent)
 
 
 def out_product(core, spot, rows, weights):
@@ -181,9 +184,10 @@
 
     core = lax.axis_index("c").reshape(1)
     swap = [(0, 1), (1, 0)]
-    own, other = query_product(core, scaled.reshape(8, 32, 1024), query_weights)
-    own, caches = lax.optimization_barrier((own, caches))
-    parts = (own + lax.ppermute(other, "c", swap)).reshape(32, 32, HD)
+    scaled = scaled.reshape(8, 32, 1024)
+    other = query_product(1 - core, scaled, query_weights)
+    parts = query_product(core, scaled, query_weights, lax.ppermute(other, "c", swap)).reshape(32, 32, HD)
+    parts, caches = lax.optimization_barrier((parts, caches))
     parts = lax.all_to_all(parts, ("y", "s", "x"), 0, 0, tiled=True).reshape(8, 4, 32, HD)
     caches = caches.reshape(8, 2, 2, IMG_TOK, HD)
     attended = attend(image_slot, marks, parts, query_gain.reshape(1, HD), caches)

time: 169 us -> 168 us (level)
    ppermute x1 -> x0, starting transfers between devices: 4.51 us -> none  [on_device(): parts = (own + lax.ppermute(other, 'c', swap)).reshape(32, 32, HD)]
    ppermute x1 -> x2, starting transfers between devices: 9.74 us -> 14 us  [on_device(): lax.ppermute(other, 'c', swap)]
    ppermute x1 -> x0, waiting for transfers between devices: 1.71 us -> none  [on_device(): parts = (own + lax.ppermute(other, 'c', swap)).reshape(32, 32, HD)]
where the time goes in v5:
time: 168 us
  blocking collectives  63.4 us (38%)
  starting transfers between devices  43.6 us (26%)
  waiting for transfers between devices  33.1 us (20%)
  between operations  14.3 us (9%)
  Pallas kernels  6.02 us (4%)
  other arithmetic  4.78 us (3%)
  local copies, waits for them, and re-layouts  2.52 us (2%)
    all_gather x2, blocking collectives, on_device(): scaled = lax.all_gather(lax.all_gather(scaled, 's'), 'y')  28.8 us
    all_gather x1, blocking collectives, on_device(): lax.all_gather(attended, 'j')  26 us
    ppermute x2, starting transfers between devices, on_device(): lax.ppermute(other, 'c', swap)  14 us
    all_gather x1, waiting for transfers between devices, on_device(): query_weights = lax.all_gather(w_query, 'j')  11.9 us
    all_to_all x1, starting transfers between devices, on_device(): caches = lax.all_to_all(caches, IMG, 0, 0, tiled=True)  11.5 us
    all_to_all x1, waiting for transfers between devices, on_device(): lax.all_to_all(parts, ('y', 's', 'x'), 0, 0, tiled=True)  10.1 us
    all_gather x1, blocking collectives, on_device(): out_weights = [lax.all_gather(w_out, 's')]  8.54 us
    ppermute x3, starting transfers between devices, on_device(): lax.ppermute(out_weights[0], 'y', [(a, (a + ahead) % 4) for a in range(4)])  8.4 us
  transfers between devices with their start and end apart: 9, of which 5 were waited for; matrix products, arithmetic and copies ran while one was open for 3% of the time, Pallas kernels for 1%

profile of v5, /device:TPU:1, one launch (start us, length us, event | category | flops | bytes accessed | tf_op | source)
XLA Modules:
  0.0 167.6 jit_solution(2833018007872297173)
XLA Ops:
  6.5 0.0 all-gather.7.cloned.1.call-start
  6.5 0.7 all-gather.7.cloned.1.call-update
  7.3 3.9 %bitcast_bitcast_fusion = bf16[8,2,1024,128]{3,2,1,0:T(8,128)(2,1)} fusion(bf16[1,1024,1024]{2,1,0:T(8,128)(2,1)} %param.16, bf16[1,1024,1024]{2,1,0:T(8,128)(2,1)} %param.15), kind=kLoop, calls=%fused_computation | loop fusion | flops 2097152 | bytes 8388608 | tf_op jit(solution)/shard_map/transpose | solution.py:172
  11.2 0.0 copy-start.3
  11.2 0.0 copy-start.4
  11.2 0.0 copy-start.5
  11.2 0.0 copy-start.8
  11.2 0.0 copy-start.6
  11.2 11.5 %all-to-all-start = ((bf16[8,2,1024,128]{3,2,1,0:T(8,128)(2,1)}), bf16[8,2,1024,128]{3,2,1,0:T(8,128)(2,1)}, u32[]{:S(2)}, u32[]{:S(2)}) async-start(bf16[8,2,1024,128]{3,2,1,0:T(8,128)(2,1)} %bitcast_bitcast_fusion), calls=%async_computation | async-start | bytes 8388608 | tf_op jit(solution)/shard_map/all_to_all | solution.py:174
  22.7 0.0 copy-done.3
  22.7 8.5 %all-gather.2 = bf16[2048,128]{1,0:T(8,128)(2,1)S(1)} all-gather(bf16[1024,128]{1,0:T(8,128)(2,1)S(1)} %copy-done.3), channel_id=4, replica_groups=mesh['j'=8,'s'=2,'y'=4,'x'=4,'c'=2] {'s'}, dimensions={0}, use_global_device_ids=true | all-gather | bytes 786432 | tf_op jit(solution)/shard_map/all_gather | solution.py:177
  31.2 1.9 %collective-permute-start = (bf16[2,1024,128]{2,1,0:T(8,128)(2,1)S(1)}, bf16[2,1024,128]{2,1,0:T(8,128)(2,1)S(1)}, u32[]{:S(2)}, u32[]{:S(2)}) collective-permute-start(bf16[2,1024,128]{2,1,0:T(8,128)(2,1)S(1)} %bitcast.32), channel_id=1, source_target_pairs={{0,8},{8,16},{16,24},{24,0},{1,9},{9,17},{17,25},{25,1},{2,10},{10... | collective-permute-start | bytes 1572872 | tf_op jit(solution)/shard_map/ppermute | solution.py:179
  33.1 1.9 %collective-permute-start.1 = (bf16[2,1024,128]{2,1,0:T(8,128)(2,1)S(1)}, bf16[2,1024,128]{2,1,0:T(8,128)(2,1)S(1)}, u32[]{:S(2)}, u32[]{:S(2)}) collective-permute-start(bf16[2,1024,128]{2,1,0:T(8,128)(2,1)S(1)} %bitcast.33), channel_id=1, source_target_pairs={{0,16},{8,24},{16,0},{24,8},{1,17},{9,25},{17,1},{25,9},{2,18},{10... | collective-permute-start | bytes 1572872 | tf_op jit(solution)/shard_map/ppermute | solution.py:179
  35.0 4.6 %collective-permute-start.2 = (bf16[2,1024,128]{2,1,0:T(8,128)(2,1)S(1)}, bf16[2,1024,128]{2,1,0:T(8,128)(2,1)S(1)}, u32[]{:S(2)}, u32[]{:S(2)}) collective-permute-start(bf16[2,1024,128]{2,1,0:T(8,128)(2,1)S(1)} %bitcast.34), channel_id=1, source_target_pairs={{0,24},{8,0},{16,8},{24,16},{1,25},{9,1},{17,9},{25,17},{2,26},{10... | collective-permute-start | bytes 1572872 | tf_op jit(solution)/shard_map/ppermute | solution.py:179
  39.6 0.0 copy-done.4
  39.6 0.0 copy-done.5
  39.7 6.1 %all-gather = bf16[64,1024]{1,0:T(8,128)(2,1)S(1)} all-gather(bf16[32,1024]{1,0:T(8,128)(2,1)S(1)} %multiply_convert_fusion.1), channel_id=2, replica_groups=mesh['j'=8,'s'=2,'y'=4,'x'=4,'c'=2] {'s'}, dimensions={0}, use_global_device_ids=true | all-gather | bytes 196608 | tf_op jit(solution)/shard_map/all_gather | solution.py:176
  45.8 0.0 copy-done.8
  45.8 0.0 copy-start.2
  45.8 22.7 %all-gather.1 = bf16[8,32,1024]{2,1,0:T(8,128)(2,1)S(1)} all-gather(bf16[2,32,1024]{2,1,0:T(8,128)(2,1)S(1)} %bitcast.40), channel_id=3, replica_groups=mesh['j'=8,'s'=2,'y'=4,'x'=4,'c'=2] {'y'}, dimensions={0}, use_global_device_ids=true | all-gather | bytes 655360 | tf_op jit(solution)/shard_map/all_gather | solution.py:176
  68.5 0.0 copy-done.6
  68.5 0.1 copy.24
  68.6 0.1 copy.25
  68.7 0.0 collective-permute-done.refs_1_
  68.7 0.0 collective-permute-done.1.refs_2_
  68.7 0.0 collective-permute-done.2.refs_3_
  68.7 11.9 %all-gather.7.cloned.1.call-done = bf16[8192,128]{1,0:T(8,128)(2,1)} async-done(((bf16[1024,128]{1,0:T(8,128)(2,1)}), bf16[8192,128]{1,0:T(8,128)(2,1)}) %all-gather.7.cloned.1.call-update) | async-done | bytes 2097168 | tf_op jit(solution)/shard_map/all_gather | solution.py:171
  80.6 1.6 copy-done
  82.2 0.4 shard_map.109
  82.7 4.3 %collective-permute-start.3 = (f32[8,4,32,128]{3,2,1,0:T(8,128)S(1)}, f32[8,4,32,128]{3,2,1,0:T(8,128)S(1)}, u32[]{:S(2)}, u32[]{:S(2)}) collective-permute-start(f32[8,4,32,128]{3,2,1,0:T(8,128)S(1)} %shard_map.109), channel_id=1, source_target_pairs={{0,1},{1,0},{2,3},{3,2},{4,5},{5,4},{6,7},{7,6},{8,9},{9,8},{10,11... | collective-permute-start | bytes 1572872 | tf_op jit(solution)/shard_map/ppermute | solution.py:189
  87.0 1.5 collective-permute-done.3.refs_0_
  88.5 0.0 copy-done.1
  88.5 1.3 shard_map.110
  89.8 0.0 all-to-all-done
  89.8 5.5 %all-to-all-start.1 = ((f32[32,32,128]{2,1,0:T(8,128)}), f32[32,32,128]{2,1,0:T(8,128)S(1)}, u32[]{:S(2)}, u32[]{:S(2)}) async-start(f32[32,32,128]{2,1,0:T(8,128)} %bitcast.12), calls=%async_computation.1 | async-start | bytes 1048576 | tf_op jit(solution)/shard_map/all_to_all | solution.py:191
  95.3 0.0 copy-done.7
  95.3 0.1 copy.26.slots_ref
  95.4 10.1 %all-to-all-done.1 = f32[32,32,128]{2,1,0:T(8,128)S(1)} async-done(((f32[32,32,128]{2,1,0:T(8,128)}), f32[32,32,128]{2,1,0:T(8,128)S(1)}, u32[]{:S(2)}, u32[]{:S(2)}) %all-to-all-start.1) | async-done | bytes 524320 | tf_op jit(solution)/shard_map/all_to_all | solution.py:191
  105.5 0.0 copy-done.2
  105.5 3.6 %shard_map.111 = bf16[32,1024]{1,0:T(8,128)(2,1)S(1)} custom-call(s32[8,2]{1,0:T(8,128)S(1)} %copy.26.slots_ref, f32[64,8]{1,0:T(8,128)S(1)} %bitcast.38, f32[8,4,32,128]{3,2,1,0:T(8,128)S(1)} %bitcast.36, f32[1,128]{1,0:T(1,128)S(1)} %bitcast.39, bf16[8,2,2,512,128]{4,3,2,1,0:T(8,128)(2,1)} %bitcast.15.cache_ref), custom_call_target="tpu_custom_call" | custom-call | flops 134217728 | bytes 5242880 | tf_op jit(solution)/shard_map/pallas_call | solution.py:147
  109.0 26.0 %all-gather.4 = bf16[256,1024]{1,0:T(8,128)(2,1)S(1)} all-gather(bf16[32,1024]{1,0:T(8,128)(2,1)S(1)} %shard_map.111), channel_id=6, replica_groups=mesh['j'=8,'s'=2,'y'=4,'x'=4,'c'=2] {'j'}, dimensions={0}, use_global_device_ids=true | all-gather | bytes 589824 | tf_op jit(solution)/shard_map/all_gather | solution.py:196
  135.1 0.7 shard_map.112
  135.8 9.7 %collective-permute-start.4 = (f32[4,2,4,32,128]{4,3,2,1,0:T(8,128)S(1)}, f32[4,2,4,32,128]{4,3,2,1,0:T(8,128)S(1)}, u32[]{:S(2)}, u32[]{:S(2)}) collective-permute-start(f32[4,2,4,32,128]{4,3,2,1,0:T(8,128)S(1)} %get-tuple-element.28), channel_id=1, source_target_pairs={{0,1},{1,0},{2,3},{3,2},{4,5},{5,4},{6,7},{7,6},{8,9},{9,8},{10,11... | collective-permute-start | bytes 1572872 | tf_op jit(solution)/shard_map/ppermute | solution.py:197
  145.5 1.5 collective-permute-done.4
  147.0 0.8 add_convert_fusion
  147.8 4.3 %all-to-all-start.2 = ((bf16[32,32,128]{2,1,0:T(8,128)(2,1)}), bf16[32,32,128]{2,1,0:T(8,128)(2,1)S(1)}, u32[]{:S(2)}, u32[]{:S(2)}) async-start(bf16[32,32,128]{2,1,0:T(8,128)(2,1)} %bitcast.17), calls=%async_computation.2 | async-start | bytes 524288 | tf_op jit(solution)/shard_map/all_to_all | solution.py:198
  152.8 7.3 %all-to-all-done.2 = bf16[32,32,128]{2,1,0:T(8,128)(2,1)S(1)} async-done(((bf16[32,32,128]{2,1,0:T(8,128)(2,1)}), bf16[32,32,128]{2,1,0:T(8,128)(2,1)S(1)}, u32[]{:S(2)}, u32[]{:S(2)}) %all-to-all-start.2) | async-done | bytes 262176 | tf_op jit(solution)/shard_map/all_to_all | solution.py:198
  160.1 0.6 copy.27
  (11 shorter events, 0.1 us)
Async XLA Ops:
  6.5 74.1 %all-gather.7.cloned.1.call-start = ((), (), s32[]{:S(2)}) async-start(), calls=%async_computation.3 | async-start | bytes 2359296 | tf_op jit(solution)/shard_map/all_gather | solution.py:171
  11.2 11.5 %copy-start.3 = (bf16[1024,128]{1,0:T(8,128)(2,1)S(1)}, bf16[1024,128]{1,0:T(8,128)(2,1)}, u32[]{:S(2)}) copy-start(bf16[1024,128]{1,0:T(8,128)(2,1)} %param.21) | copy-start | bytes 786436
  11.2 28.5 %copy-start.4 = (bf16[32,1024]{1,0:T(8,128)(2,1)S(1)}, bf16[32,1024]{1,0:T(8,128)(2,1)}, u32[]{:S(2)}) copy-start(bf16[32,1024]{1,0:T(8,128)(2,1)} %param.11) | copy-start | bytes 196612
  11.2 28.5 %copy-start.5 = (f32[1024]{0:T(1024)S(1)}, f32[1024]{0:T(1024)}, u32[]{:S(2)}) copy-start(f32[1024]{0:T(1024)} %param.12) | copy-start | bytes 12292
  11.2 34.6 %copy-start.8 = (s32[8]{0:T(128)S(1)}, s32[8]{0:T(128)}, u32[]{:S(2)}) copy-start(s32[8]{0:T(128)} %param.18) | copy-start | bytes 100
  11.2 57.3 %copy-start.6 = (s32[32,8]{0,1:T(8,128)S(1)}, s32[32,8]{0,1:T(8,128)}, u32[]{:S(2)}) copy-start(s32[32,8]{0,1:T(8,128)} %param.17) | copy-start | bytes 3076
  11.2 78.6 %all-to-all-start = ((bf16[8,2,1024,128]{3,2,1,0:T(8,128)(2,1)}), bf16[8,2,1024,128]{3,2,1,0:T(8,128)(2,1)}, u32[]{:S(2)}, u32[]{:S(2)}) async-start(bf16[8,2,1024,128]{3,2,1,0:T(8,128)(2,1)} %bitcast_bitcast_fusion), calls=%async_computation | async-start | bytes 8388608 | tf_op jit(solution)/shard_map/all_to_all | solution.py:174
  31.2 37.5 %collective-permute-start = (bf16[2,1024,128]{2,1,0:T(8,128)(2,1)S(1)}, bf16[2,1024,128]{2,1,0:T(8,128)(2,1)S(1)}, u32[]{:S(2)}, u32[]{:S(2)}) collective-permute-start(bf16[2,1024,128]{2,1,0:T(8,128)(2,1)S(1)} %bitcast.32), channel_id=1, source_target_pairs={{0,8},{8,16},{16,24},{24,0},{1,9},{9,17},{17,25},{25,1},{2,10},{10... | collective-permute-start | bytes 1572872 | tf_op jit(solution)/shard_map/ppermute | solution.py:179
  33.1 35.6 %collective-permute-start.1 = (bf16[2,1024,128]{2,1,0:T(8,128)(2,1)S(1)}, bf16[2,1024,128]{2,1,0:T(8,128)(2,1)S(1)}, u32[]{:S(2)}, u32[]{:S(2)}) collective-permute-start(bf16[2,1024,128]{2,1,0:T(8,128)(2,1)S(1)} %bitcast.33), channel_id=1, source_target_pairs={{0,16},{8,24},{16,0},{24,8},{1,17},{9,25},{17,1},{25,9},{2,18},{10... | collective-permute-start | bytes 1572872 | tf_op jit(solution)/shard_map/ppermute | solution.py:179
  35.0 33.7 %collective-permute-start.2 = (bf16[2,1024,128]{2,1,0:T(8,128)(2,1)S(1)}, bf16[2,1024,128]{2,1,0:T(8,128)(2,1)S(1)}, u32[]{:S(2)}, u32[]{:S(2)}) collective-permute-start(bf16[2,1024,128]{2,1,0:T(8,128)(2,1)S(1)} %bitcast.34), channel_id=1, source_target_pairs={{0,24},{8,0},{16,8},{24,16},{1,25},{9,1},{17,9},{25,17},{2,26},{10... | collective-permute-start | bytes 1572872 | tf_op jit(solution)/shard_map/ppermute | solution.py:179
  45.8 49.5 %copy-start.7 = (s32[8,2]{0,1:T(2,128)S(1)}, s32[8,2]{0,1:T(2,128)}, u32[]{:S(2)}) copy-start(s32[8,2]{0,1:T(2,128)} %param.19) | copy-start | bytes 196
  45.8 59.7 %copy-start.2 = (f32[128]{0:T(128)S(1)}, f32[128]{0:T(128)}, u32[]{:S(2)}) copy-start(f32[128]{0:T(128)} %param.14) | copy-start | bytes 1540
  80.6 1.6 copy-start
  82.2 6.2 %copy-start.1 = (bf16[8192,128]{1,0:T(8,128)(2,1)S(1)}, bf16[8192,128]{1,0:T(8,128)(2,1)}, u32[]{:S(2)}) copy-start(bf16[8192,128]{1,0:T(8,128)(2,1)} %all-gather.7.cloned.1.call-done) | copy-start | bytes 6291460
  82.7 5.8 %collective-permute-start.3 = (f32[8,4,32,128]{3,2,1,0:T(8,128)S(1)}, f32[8,4,32,128]{3,2,1,0:T(8,128)S(1)}, u32[]{:S(2)}, u32[]{:S(2)}) collective-permute-start(f32[8,4,32,128]{3,2,1,0:T(8,128)S(1)} %shard_map.109), channel_id=1, source_target_pairs={{0,1},{1,0},{2,3},{3,2},{4,5},{5,4},{6,7},{7,6},{8,9},{9,8},{10,11... | collective-permute-start | bytes 1572872 | tf_op jit(solution)/shard_map/ppermute | solution.py:189
  89.8 15.7 %all-to-all-start.1 = ((f32[32,32,128]{2,1,0:T(8,128)}), f32[32,32,128]{2,1,0:T(8,128)S(1)}, u32[]{:S(2)}, u32[]{:S(2)}) async-start(f32[32,32,128]{2,1,0:T(8,128)} %bitcast.12), calls=%async_computation.1 | async-start | bytes 1048576 | tf_op jit(solution)/shard_map/all_to_all | solution.py:191
  135.8 11.2 %collective-permute-start.4 = (f32[4,2,4,32,128]{4,3,2,1,0:T(8,128)S(1)}, f32[4,2,4,32,128]{4,3,2,1,0:T(8,128)S(1)}, u32[]{:S(2)}, u32[]{:S(2)}) collective-permute-start(f32[4,2,4,32,128]{4,3,2,1,0:T(8,128)S(1)} %get-tuple-element.28), channel_id=1, source_target_pairs={{0,1},{1,0},{2,3},{3,2},{4,5},{5,4},{6,7},{7,6},{8,9},{9,8},{10,11... | collective-permute-start | bytes 1572872 | tf_op jit(solution)/shard_map/ppermute | solution.py:197
  147.8 12.3 %all-to-all-start.2 = ((bf16[32,32,128]{2,1,0:T(8,128)(2,1)}), bf16[32,32,128]{2,1,0:T(8,128)(2,1)S(1)}, u32[]{:S(2)}, u32[]{:S(2)}) async-start(bf16[32,32,128]{2,1,0:T(8,128)(2,1)} %bitcast.17), calls=%async_computation.2 | async-start | bytes 524288 | tf_op jit(solution)/shard_map/all_to_all | solution.py:198
Sparse Core Ops, SparseCore 0:
  9.4 71.1 all-gather.6
